TPU v7x, 256 devices: a whole 4x4x8 slice. The times are simulated.
256 devices in a mesh: pipe: 4 (over z_lo, core), fsdp: 64 (over x, z_hi, y).
Axes of the slice: x: 4, y: 4, z: 8 (z_hi: 4, z_lo: 2; z = z_hi * 2 + z_lo), core: 2. Of those that a mesh axis runs over, the one named last changes fastest.
Arguments:
- tokens: int32 [2, 160], replicated, may hold values from 0 to 511
- embed: bfloat16 [512, 8192], P(None, 'fsdp'), may hold values from -60 to 60
- gain: bfloat16 [4, 8192], P('pipe', 'fsdp'), may hold values from 0.099609375 to 1.8984375
- w_in: bfloat16 [4, 3, 8192, 8192], P('pipe', None, None, 'fsdp'), may hold values from -0.0625 to 0.0625
- short_filter: float32 [4, 3, 7, 8192], P('pipe', None, None, 'fsdp'), may hold values from -2 to 2
- long_filter: float32 [4, 512, 128], P('pipe', 'fsdp'), may hold values from -0.5 to 0.5
- skip_bias: float32 [4, 8192], P('pipe', 'fsdp'), may hold values from -1 to 1
- w_out: bfloat16 [4, 8192, 8192], P('pipe', None, 'fsdp'), may hold values from -0.0625 to 0.0625
Outputs:
- hidden: bfloat16 [2, 160, 8192], P(None, 'pipe', 'fsdp')
All inputs are finite; a program needn't handle non-finite values.
Results may differ from a plain program's by a relative error of at most 0.035.
Values may be sent and summed in bfloat16 or wider, within the bound.
No kernel may reach another device: no remote copies, remote signals or barrier semaphores. Data moves between devices by JAX's collectives and lax.ppermute only.
A program may use at most 64 MiB of HBM per device.

v0:
```python
import jax
import jax.numpy as jnp
from jax import lax
from jax.sharding import PartitionSpec as P

D = 8192
GROUP = 16


def from_behind(block, axis, distance):
    devices = range(lax.axis_size(axis))
    route = [(i - distance, i) for i in devices if i - distance in devices]
    return lax.ppermute(block, axis, route)


def spread(value, axis, root):
    mine = lax.axis_index(axis) == root
    return lax.psum(jnp.where(mine, value, jnp.zeros_like(value)), axis)


def short_mix(projected, filters):
    width = filters.shape[1]
    seq_len = projected.shape[1]
    padded = jnp.pad(projected.astype(jnp.float32), ((0, 0), (width - 1, 0), (0, 0)))
    running = jnp.zeros(projected.shape, jnp.float32)
    for offset in range(width):
        window = padded[:, width - 1 - offset : width - 1 - offset + seq_len, :]
        running = running + filters[:, offset][:, None, :] * window
    return running


def long_mix(signal, kernels, group_size):
    seq_len = signal.shape[0]
    span = kernels.shape[1]
    count_filters = kernels.shape[0]
    positions = jnp.arange(seq_len, dtype=jnp.int32)
    lag_table = positions[:, None] - positions[None, :]
    inside = (lag_table >= 0) & (lag_table < span)
    lag_index = jnp.clip(lag_table, 0, span - 1)
    toeplitz = jnp.where(inside[None, :, :], kernels[:, lag_index], jnp.float32(0.0))
    grouped = signal.reshape(seq_len, count_filters, group_size)
    mixed = jnp.einsum("fts,sfg->tfg", toeplitz, grouped, precision=lax.Precision.HIGHEST)
    return mixed.reshape(seq_len, count_filters * group_size)


def body(tokens, embed, gain, w_in, short_filter, long_filter, skip_bias, w_out):
    segment_count = lax.axis_size("pipe")
    segment_index = lax.axis_index("pipe")
    batch_count = tokens.shape[0]
    seq_len = tokens.shape[1]
    local_width = embed.shape[1]
    in_weights = w_in[0]
    short_taps = short_filter[0]
    long_taps = long_filter[0]
    skip_row = skip_bias[0]
    out_weight = w_out[0]
    vocab_index = jnp.arange(embed.shape[0], dtype=jnp.int32)

    def layer_step(activation):
        widened = activation.astype(jnp.float32)
        squares = lax.psum(jnp.sum(widened * widened, axis=1), "fsdp")
        inverse_rms = lax.rsqrt(squares / D + 1e-06)[:, None]
        normalized = (widened * inverse_rms * gain.astype(jnp.float32)).astype(jnp.bfloat16)
        weight_rows = in_weights
        projected = jnp.einsum(
            "sk,jkc->jsc",
            lax.all_gather(normalized, "fsdp", axis=1, tiled=True),
            weight_rows,
            preferred_element_type=jnp.float32,
        )
        mixed = short_mix(projected.astype(jnp.bfloat16), short_taps)
        product = mixed[1] * mixed[2]
        carried = long_mix(product, long_taps, GROUP) + skip_row[None, :] * product
        gated = (mixed[0] * carried).astype(jnp.bfloat16)
        weight_rows = out_weight
        projected_out = jnp.dot(
            lax.all_gather(gated, "fsdp", axis=1, tiled=True),
            weight_rows,
            preferred_element_type=jnp.float32,
        )
        return (widened + projected_out).astype(jnp.bfloat16)

    def tick_body(tick_index, carry_state):
        previous, collected = carry_state
        incoming = from_behind(previous, "pipe", 1)
        micro_index = tick_index - segment_index
        chosen = jnp.clip(micro_index, 0, batch_count - 1)
        token_ids = lax.dynamic_index_in_dim(tokens, chosen, 0, keepdims=False)
        one_hot = (token_ids[:, None] == vocab_index[None, :]).astype(jnp.bfloat16)
        embedded = jnp.dot(one_hot, embed, preferred_element_type=jnp.float32).astype(jnp.bfloat16)
        activation = jnp.where(segment_index == 0, embedded, incoming)
        layer_out = layer_step(activation)
        store_flag = (
            (micro_index >= 0) & (micro_index < batch_count) & (segment_index == segment_count - 1)
        )
        updated = lax.dynamic_update_index_in_dim(collected, layer_out, chosen, 0)
        collected = jnp.where(store_flag, updated, collected)
        return (layer_out, collected)

    start_state = (
        jnp.zeros((seq_len, local_width), jnp.bfloat16),
        jnp.zeros((batch_count, seq_len, local_width), jnp.bfloat16),
    )
    final_state = lax.fori_loop(0, batch_count + segment_count - 1, tick_body, start_state)
    finished = spread(final_state[1], "pipe", segment_count - 1)
    row_share = seq_len // segment_count
    return lax.dynamic_slice_in_dim(finished, segment_index * row_share, row_share, 1)


def solution(mesh):
    return jax.shard_map(
        body,
        mesh=mesh,
        in_specs=(
            P(),
            P(None, "fsdp"),
            P("pipe", "fsdp"),
            P("pipe", None, None, "fsdp"),
            P("pipe", None, None, "fsdp"),
            P("pipe", "fsdp", None),
            P("pipe", "fsdp"),
            P("pipe", None, "fsdp"),
        ),
        out_specs=P(None, "pipe", "fsdp"),
        check_vma=False,
    )
```

profile of v0, /device:TPU:1, one launch (start us, length us, event | category | flops | bytes accessed | tf_op | source)
XLA Modules:
  0.0 2043.1 jit_solution(8263287136697875596)
XLA Ops:
  10.1 1982.0 %while.18 = (s32[]{:T(128)}, bf16[160,128]{1,0:T(8,128)(2,1)}, bf16[2,160,128]{2,1,0:T(8,128)(2,1)}, pred[]{:T(512)}, s32[]{:T(128)}, /*index=5*/s32[2,160]{1,0:...) while((s32[]{:T(128)}, bf16[160,128]{1,0:T(8,128)(2,1)}, ...), condition=%wide.region_3.4_spmd.clone, body=%wide.region_0.3_spmd.clone.sunk | while | flops 1404303872 | bytes 46493152 | solution.py:104
  17.7 168.4 %psum.24 = f32[160]{0:T(256)S(1)} all-reduce(f32[160]{0:T(256)S(1)} %get-tuple-element.508), channel_id=1, replica_groups=mesh['pipe'=4,'fsdp'=64] {'fsdp'}, use_global_device_ids=true, to_apply=%region_2.2 | all-reduce | flops 160 | bytes 1280 | tf_op jit(solution)/shard_map/while/body/eval_jaxpr/psum | solution.py:61
  187.1 85.3 %gather_fusion = f32[25600,8]{1,0:T(8,128)} fusion(f32[8,128]{0,1:T(8,128)S(1)} %get-tuple-element.562, s32[25600]{0:T(1024)S(1)} %broadcast_clamp_fusion.2), kind=kCustom, calls=%fused_computation.clone.clone.1 | custom fusion | bytes 1740800 | tf_op jit(solution)/shard_map/while/body/eval_jaxpr/gather | solution.py:40
  272.4 8.8 copy.25
  283.2 13.5 all-gather.3.cloned.1.call-done
  296.7 5.1 fusion.56
  310.4 96.4 %all-gather.5.cloned.1.call-done = bf16[160,8192]{1,0:T(8,128)(2,1)} async-done(((bf16[160,128]{1,0:T(8,128)(2,1)}), bf16[160,8192]{1,0:T(8,128)(2,1)}) %all-gather.5.cloned.1.call-update) | async-done | bytes 2621456 | tf_op jit(solution)/shard_map/while/body/eval_jaxpr/all_gather | solution.py:77
  415.4 166.0 %psum.24 = f32[160]{0:T(256)S(1)} all-reduce(f32[160]{0:T(256)S(1)} %get-tuple-element.508), channel_id=1, replica_groups=mesh['pipe'=4,'fsdp'=64] {'fsdp'}, use_global_device_ids=true, to_apply=%region_2.2 | all-reduce | flops 160 | bytes 1280 | tf_op jit(solution)/shard_map/while/body/eval_jaxpr/psum | solution.py:61
  582.4 85.3 %gather_fusion = f32[25600,8]{1,0:T(8,128)} fusion(f32[8,128]{0,1:T(8,128)S(1)} %get-tuple-element.562, s32[25600]{0:T(1024)S(1)} %broadcast_clamp_fusion.2), kind=kCustom, calls=%fused_computation.clone.clone.1 | custom fusion | bytes 1740800 | tf_op jit(solution)/shard_map/while/body/eval_jaxpr/gather | solution.py:40
  667.6 8.8 copy.25
  678.5 13.8 all-gather.3.cloned.1.call-done
  692.3 5.1 fusion.56
  706.1 96.3 %all-gather.5.cloned.1.call-done = bf16[160,8192]{1,0:T(8,128)(2,1)} async-done(((bf16[160,128]{1,0:T(8,128)(2,1)}), bf16[160,8192]{1,0:T(8,128)(2,1)}) %all-gather.5.cloned.1.call-update) | async-done | bytes 2621456 | tf_op jit(solution)/shard_map/while/body/eval_jaxpr/all_gather | solution.py:77
  810.9 166.0 %psum.24 = f32[160]{0:T(256)S(1)} all-reduce(f32[160]{0:T(256)S(1)} %get-tuple-element.508), channel_id=1, replica_groups=mesh['pipe'=4,'fsdp'=64] {'fsdp'}, use_global_device_ids=true, to_apply=%region_2.2 | all-reduce | flops 160 | bytes 1280 | tf_op jit(solution)/shard_map/while/body/eval_jaxpr/psum | solution.py:61
  977.9 85.3 %gather_fusion = f32[25600,8]{1,0:T(8,128)} fusion(f32[8,128]{0,1:T(8,128)S(1)} %get-tuple-element.562, s32[25600]{0:T(1024)S(1)} %broadcast_clamp_fusion.2), kind=kCustom, calls=%fused_computation.clone.clone.1 | custom fusion | bytes 1740800 | tf_op jit(solution)/shard_map/while/body/eval_jaxpr/gather | solution.py:40
  1063.1 8.8 copy.25
  1074.0 13.8 all-gather.3.cloned.1.call-done
  1087.8 5.1 fusion.56
  1101.6 96.3 %all-gather.5.cloned.1.call-done = bf16[160,8192]{1,0:T(8,128)(2,1)} async-done(((bf16[160,128]{1,0:T(8,128)(2,1)}), bf16[160,8192]{1,0:T(8,128)(2,1)}) %all-gather.5.cloned.1.call-update) | async-done | bytes 2621456 | tf_op jit(solution)/shard_map/while/body/eval_jaxpr/all_gather | solution.py:77
  1206.4 166.0 %psum.24 = f32[160]{0:T(256)S(1)} all-reduce(f32[160]{0:T(256)S(1)} %get-tuple-element.508), channel_id=1, replica_groups=mesh['pipe'=4,'fsdp'=64] {'fsdp'}, use_global_device_ids=true, to_apply=%region_2.2 | all-reduce | flops 160 | bytes 1280 | tf_op jit(solution)/shard_map/while/body/eval_jaxpr/psum | solution.py:61
  1373.4 85.3 %gather_fusion = f32[25600,8]{1,0:T(8,128)} fusion(f32[8,128]{0,1:T(8,128)S(1)} %get-tuple-element.562, s32[25600]{0:T(1024)S(1)} %broadcast_clamp_fusion.2), kind=kCustom, calls=%fused_computation.clone.clone.1 | custom fusion | bytes 1740800 | tf_op jit(solution)/shard_map/while/body/eval_jaxpr/gather | solution.py:40
  1458.6 8.8 copy.25
  1469.5 13.8 all-gather.3.cloned.1.call-done
  1483.3 5.1 fusion.56
  1497.1 96.3 %all-gather.5.cloned.1.call-done = bf16[160,8192]{1,0:T(8,128)(2,1)} async-done(((bf16[160,128]{1,0:T(8,128)(2,1)}), bf16[160,8192]{1,0:T(8,128)(2,1)}) %all-gather.5.cloned.1.call-update) | async-done | bytes 2621456 | tf_op jit(solution)/shard_map/while/body/eval_jaxpr/all_gather | solution.py:77
  1601.9 166.0 %psum.24 = f32[160]{0:T(256)S(1)} all-reduce(f32[160]{0:T(256)S(1)} %get-tuple-element.508), channel_id=1, replica_groups=mesh['pipe'=4,'fsdp'=64] {'fsdp'}, use_global_device_ids=true, to_apply=%region_2.2 | all-reduce | flops 160 | bytes 1280 | tf_op jit(solution)/shard_map/while/body/eval_jaxpr/psum | solution.py:61
  1768.9 85.3 %gather_fusion = f32[25600,8]{1,0:T(8,128)} fusion(f32[8,128]{0,1:T(8,128)S(1)} %get-tuple-element.562, s32[25600]{0:T(1024)S(1)} %broadcast_clamp_fusion.2), kind=kCustom, calls=%fused_computation.clone.clone.1 | custom fusion | bytes 1740800 | tf_op jit(solution)/shard_map/while/body/eval_jaxpr/gather | solution.py:40
  1854.1 8.8 copy.25
  1865.0 13.8 all-gather.3.cloned.1.call-done
  1878.8 5.1 fusion.56
  1892.6 96.3 %all-gather.5.cloned.1.call-done = bf16[160,8192]{1,0:T(8,128)(2,1)} async-done(((bf16[160,128]{1,0:T(8,128)(2,1)}), bf16[160,8192]{1,0:T(8,128)(2,1)}) %all-gather.5.cloned.1.call-update) | async-done | bytes 2621456 | tf_op jit(solution)/shard_map/while/body/eval_jaxpr/all_gather | solution.py:77
  1992.7 41.6 %all-reduce.3.cloned.1.call-done = bf16[2,160,128]{2,1,0:T(8,128)(2,1)} async-done(((bf16[2,160,128]{2,1,0:T(8,128)(2,1)}), bf16[2,160,128]{2,1,0:T(8,128)(2,1)}) %all-reduce.3.cloned.1.call-update) | async-done | bytes 81936 | tf_op jit(solution)/shard_map/psum | solution.py:18
  (218 shorter events, 107.4 us)
Async XLA Ops:
  10.1 286.6 %all-gather.3.cloned.1.call-start = ((), (), s32[]{:S(2)}) async-start(), calls=%async_computation.1 | async-start | bytes 2662400 | tf_op jit(solution)/shard_map/while/body/eval_jaxpr/all_gather | solution.py:67
  10.1 6.3 collective-permute-start
  186.8 220.0 %all-gather.5.cloned.1.call-start = ((), (), s32[]{:S(2)}) async-start(), calls=%async_computation.2 | async-start | bytes 2662400 | tf_op jit(solution)/shard_map/while/body/eval_jaxpr/all_gather | solution.py:77
  296.7 5.2 copy-start.7
  296.7 5.2 copy-start.8
  301.8 105.1 %copy-start = (bf16[8192,128]{1,0:T(8,128)(2,1)S(1)}, bf16[8192,128]{1,0:T(8,128)(2,1)}, u32[]{:S(2)}) copy-start(bf16[8192,128]{1,0:T(8,128)(2,1)} %get-tuple-element.564) | copy-start | bytes 6291460 | tf_op jit(solution)/shard_map/while
  410.1 282.2 %all-gather.3.cloned.1.call-start = ((), (), s32[]{:S(2)}) async-start(), calls=%async_computation.1 | async-start | bytes 2662400 | tf_op jit(solution)/shard_map/while/body/eval_jaxpr/all_gather | solution.py:67
  410.9 3.3 collective-permute-start
  582.1 220.2 %all-gather.5.cloned.1.call-start = ((), (), s32[]{:S(2)}) async-start(), calls=%async_computation.2 | async-start | bytes 2662400 | tf_op jit(solution)/shard_map/while/body/eval_jaxpr/all_gather | solution.py:77
  692.3 5.2 copy-start.6
  692.3 5.2 copy-start.7
  692.3 5.2 copy-start.8
  697.4 104.9 %copy-start = (bf16[8192,128]{1,0:T(8,128)(2,1)S(1)}, bf16[8192,128]{1,0:T(8,128)(2,1)}, u32[]{:S(2)}) copy-start(bf16[8192,128]{1,0:T(8,128)(2,1)} %get-tuple-element.564) | copy-start | bytes 6291460 | tf_op jit(solution)/shard_map/while
  805.6 282.2 %all-gather.3.cloned.1.call-start = ((), (), s32[]{:S(2)}) async-start(), calls=%async_computation.1 | async-start | bytes 2662400 | tf_op jit(solution)/shard_map/while/body/eval_jaxpr/all_gather | solution.py:67
  806.4 3.3 collective-permute-start
  977.6 220.2 %all-gather.5.cloned.1.call-start = ((), (), s32[]{:S(2)}) async-start(), calls=%async_computation.2 | async-start | bytes 2662400 | tf_op jit(solution)/shard_map/while/body/eval_jaxpr/all_gather | solution.py:77
  1087.8 5.2 copy-start.7
  1087.8 5.2 copy-start.8
  1093.0 104.9 %copy-start = (bf16[8192,128]{1,0:T(8,128)(2,1)S(1)}, bf16[8192,128]{1,0:T(8,128)(2,1)}, u32[]{:S(2)}) copy-start(bf16[8192,128]{1,0:T(8,128)(2,1)} %get-tuple-element.564) | copy-start | bytes 6291460 | tf_op jit(solution)/shard_map/while
  1201.1 282.2 %all-gather.3.cloned.1.call-start = ((), (), s32[]{:S(2)}) async-start(), calls=%async_computation.1 | async-start | bytes 2662400 | tf_op jit(solution)/shard_map/while/body/eval_jaxpr/all_gather | solution.py:67
  1201.9 3.3 collective-permute-start
  1373.1 220.2 %all-gather.5.cloned.1.call-start = ((), (), s32[]{:S(2)}) async-start(), calls=%async_computation.2 | async-start | bytes 2662400 | tf_op jit(solution)/shard_map/while/body/eval_jaxpr/all_gather | solution.py:77
  1483.3 5.2 copy-start.7
  1483.3 5.2 copy-start.8
  1488.4 104.9 %copy-start = (bf16[8192,128]{1,0:T(8,128)(2,1)S(1)}, bf16[8192,128]{1,0:T(8,128)(2,1)}, u32[]{:S(2)}) copy-start(bf16[8192,128]{1,0:T(8,128)(2,1)} %get-tuple-element.564) | copy-start | bytes 6291460 | tf_op jit(solution)/shard_map/while
  1596.6 282.2 %all-gather.3.cloned.1.call-start = ((), (), s32[]{:S(2)}) async-start(), calls=%async_computation.1 | async-start | bytes 2662400 | tf_op jit(solution)/shard_map/while/body/eval_jaxpr/all_gather | solution.py:67
  1597.4 3.3 collective-permute-start
  1768.6 220.2 %all-gather.5.cloned.1.call-start = ((), (), s32[]{:S(2)}) async-start(), calls=%async_computation.2 | async-start | bytes 2662400 | tf_op jit(solution)/shard_map/while/body/eval_jaxpr/all_gather | solution.py:77
  1878.8 5.2 copy-start.7
  1878.8 5.2 copy-start.8
  1883.9 104.9 %copy-start = (bf16[8192,128]{1,0:T(8,128)(2,1)S(1)}, bf16[8192,128]{1,0:T(8,128)(2,1)}, u32[]{:S(2)}) copy-start(bf16[8192,128]{1,0:T(8,128)(2,1)} %get-tuple-element.564) | copy-start | bytes 6291460 | tf_op jit(solution)/shard_map/while
  1992.1 42.3 %all-reduce.3.cloned.1.call-start = ((), (), s32[]{:S(2)}) async-start(), calls=%async_computation | async-start | bytes 163840 | tf_op jit(solution)/shard_map/psum | solution.py:18
  (29 other events, 127.6 us)
Sparse Core Ops, SparseCore 0:
  187.0 109.6 all-gather.2
  310.6 96.2 all-gather.4
  582.2 110.0 all-gather.2
  706.2 96.1 all-gather.4
  977.7 110.0 all-gather.2
  1101.7 96.1 all-gather.4
  1373.2 110.0 all-gather.2
  1497.2 96.1 all-gather.4
  1768.7 110.0 all-gather.2
  1892.7 96.1 all-gather.4
Sparse Core Ops, SparseCore 1:
  1995.2 39.2 all-reduce.2
where the time goes:
time: 2050 us; the launch traced here: 2040 us
  blocking collectives  832 us (41%)
  waiting for transfers between devices  592 us (29%)
  local copies, waits for them, and re-layouts  502 us (24%)
  matrix products  61.6 us (3%)
  other arithmetic  26.4 us (1%)
    psum x5, blocking collectives, layer_step(): squares = lax.psum(jnp.sum(widened * widened, axis=1), 'fsdp')  832 us
    all_gather x5, waiting for transfers between devices, layer_step(): lax.all_gather(gated, 'fsdp', axis=1, tiled=True)  482 us
    gather x10, local copies, waits for them, and re-layouts, long_mix(): kernels[:, lag_index]  470 us
    all_gather x5, waiting for transfers between devices, layer_step(): lax.all_gather(normalized, 'fsdp', axis=1, tiled=True)  68.8 us
    psum x1, waiting for transfers between devices, spread(): return lax.psum(jnp.where(mine, value, jnp.zeros_like(value)), axis)  41.6 us
  transfers between devices with their start and end apart: 16, of which 11 were waited for; matrix products, arithmetic and copies ran while one was open for 24% of the time, Pallas kernels for 0%

commit v1 on v0

v1 whole, which is shorter than its diff:
```python
import itertools

import jax
import jax.numpy as jnp
from jax import lax
from jax.experimental import pallas as pl
from jax.experimental.pallas import tpu as pltpu
from jax.sharding import PartitionSpec as P

D = 8192
STAPS = 7
SEQ = 160
LANES = 128
GROUP = 16
TABLE = 256
SIDE = 4
AXES = ("pipe", "fsdp")
PIPES = 4
FSDP = 64
EXTRA = 16
F32 = jnp.float32
BF16 = jnp.bfloat16


def place(x, z, y):
    return (x * SIDE + z) * SIDE + y


LINES_Z = [
    [p * FSDP + place(x, z, y) for z in range(SIDE)]
    for p, x, y in itertools.product(range(PIPES), range(SIDE), range(SIDE))
]
PLANES_XY = [
    [p * FSDP + place(x, z, y) for x, y in itertools.product(range(SIDE), range(SIDE))]
    for p, z in itertools.product(range(PIPES), range(SIDE))
]


def hop(value, moves):
    pairs = [(a * FSDP + f, b * FSDP + f) for a, b in moves for f in range(FSDP)]
    return lax.ppermute(value, AXES, pairs)


def share(value, groups):
    count = len(groups[0])
    copies = jnp.broadcast_to(value[None], (count,) + value.shape)
    return lax.all_to_all(copies, AXES, 0, 0, axis_index_groups=groups)


def gather_channels(block):
    return share(share(block, LINES_Z), PLANES_XY)


def toeplitz_kernel(base_ref, out_ref):
    row = lax.broadcasted_iota(jnp.int32, (SEQ, TABLE), 0)
    column = lax.broadcasted_iota(jnp.int32, (SEQ, TABLE), 1)
    for index in range(base_ref.shape[0]):
        base = jnp.broadcast_to(base_ref[index : index + 1, :], (SEQ, TABLE))
        turned = pltpu.roll(base, 0, 1, stride=1, stride_axis=0)
        out_ref[index] = jnp.where(column <= row, turned, 0.0).astype(BF16)


def toeplitz(long_taps):
    count = long_taps.shape[0]
    base = jnp.concatenate(
        [long_taps[:, :1], jnp.zeros((count, TABLE - LANES), F32), long_taps[:, :0:-1]], axis=1
    )
    return pl.pallas_call(
        toeplitz_kernel,
        out_shape=jax.ShapeDtypeStruct((count, SEQ, TABLE), BF16),
        name="toeplitz",
    )(base)


def mix_kernel(layer, x_ref, gain_ref, w_ref, taps_ref, toep_ref, out_ref, total, squares, padded):
    step = pl.program_id(0) * SIDE + pl.program_id(1)

    @pl.when(step == 0)
    def _():
        total[...] = jnp.zeros_like(total)
        squares[...] = jnp.zeros_like(squares)

    scaled = []
    power = squares[...]
    for z in range(SIDE):
        wide = x_ref[0, z].astype(F32)
        power = power + wide * wide
        gain = gain_ref[0, z].astype(F32)[layer : layer + 1, :]
        scaled.append((wide * gain).astype(BF16))
    squares[...] = power
    left = jnp.concatenate(scaled, axis=1)
    right = jnp.concatenate(
        [w_ref[0, j, 0, :, 0].reshape(SIDE * LANES, LANES) for j in range(3)], axis=1
    )
    total[...] += jnp.dot(left, right, preferred_element_type=F32)

    @pl.when(step == SIDE * SIDE - 1)
    def _():
        mean = jnp.sum(squares[...], axis=1, keepdims=True) / D
        inverse = lax.rsqrt(mean + 1e-06)
        mixed = []
        for j in range(3):
            projected = (total[:, j * LANES : (j + 1) * LANES] * inverse).astype(BF16)
            padded[j, :EXTRA] = jnp.zeros((EXTRA, LANES), F32)
            padded[j, EXTRA:] = projected.astype(F32)
            running = jnp.zeros((SEQ, LANES), F32)
            for i in range(STAPS):
                tap = taps_ref[j * STAPS + i : j * STAPS + i + 1, :]
                running = running + tap * padded[j, EXTRA - i : EXTRA - i + SEQ, :]
            mixed.append(running)
        product = mixed[1] * mixed[2]
        carried = taps_ref[3 * STAPS : 3 * STAPS + 1, :] * product
        lane = lax.broadcasted_iota(jnp.int32, (TABLE, LANES), 1)
        tall = jnp.concatenate([product, jnp.zeros((TABLE - SEQ, LANES), F32)], axis=0)
        for f in range(LANES // GROUP):
            kept = jnp.where(lane // GROUP == f, tall, 0.0).astype(BF16)
            carried = carried + jnp.dot(toep_ref[0, f], kept, preferred_element_type=F32)
        out_ref[...] = (mixed[0] * carried).astype(BF16)


def mix(layer, gathered, gains, weights, taps, toep):
    def whole(shape, first=0):
        return pl.BlockSpec(shape, lambda x, y: (first,) + (0,) * (len(shape) - 1))

    def kernel(*refs):
        mix_kernel(layer, *refs)

    filters = LANES // GROUP
    return pl.pallas_call(
        kernel,
        grid=(SIDE, SIDE),
        in_specs=[
            pl.BlockSpec((1, SIDE, SEQ, LANES), lambda x, y: (x * SIDE + y, 0, 0, 0)),
            pl.BlockSpec((1, SIDE, EXTRA, LANES), lambda x, y: (x * SIDE + y, 0, 0, 0)),
            pl.BlockSpec(
                (1, 3, 1, SIDE, 1, LANES, LANES), lambda x, y: (layer, 0, x, 0, y, 0, 0)
            ),
            whole((3 * STAPS + 3, LANES)),
            whole((1, filters, SEQ, TABLE), layer),
        ],
        out_specs=whole((SEQ, LANES)),
        out_shape=jax.ShapeDtypeStruct((SEQ, LANES), BF16),
        scratch_shapes=[
            pltpu.VMEM((SEQ, 3 * LANES), F32),
            pltpu.VMEM((SEQ, LANES), F32),
            pltpu.VMEM((3, EXTRA + SEQ, LANES), F32),
        ],
        compiler_params=pltpu.CompilerParams(vmem_limit_bytes=24 << 20),
        name="mix",
    )(gathered, gains, weights, taps, toep)


def out_kernel(g_ref, w_ref, x_ref, out_ref, total):
    step = pl.program_id(0) * SIDE + pl.program_id(1)

    @pl.when(step == 0)
    def _():
        total[...] = x_ref[...].astype(F32)

    left = jnp.concatenate([g_ref[0, z] for z in range(SIDE)], axis=1)
    right = w_ref[0, 0, :, 0].reshape(SIDE * LANES, LANES)
    total[...] += jnp.dot(left, right, preferred_element_type=F32)

    @pl.when(step == SIDE * SIDE - 1)
    def _():
        out_ref[...] = total[...].astype(BF16)


def project_out(layer, gathered, weights, activation):
    return pl.pallas_call(
        out_kernel,
        grid=(SIDE, SIDE),
        in_specs=[
            pl.BlockSpec((1, SIDE, SEQ, LANES), lambda x, y: (x * SIDE + y, 0, 0, 0)),
            pl.BlockSpec((1, 1, SIDE, 1, LANES, LANES), lambda x, y: (layer, x, 0, y, 0, 0)),
            pl.BlockSpec((SEQ, LANES), lambda x, y: (0, 0)),
        ],
        out_specs=pl.BlockSpec((SEQ, LANES), lambda x, y: (0, 0)),
        out_shape=jax.ShapeDtypeStruct((SEQ, LANES), BF16),
        scratch_shapes=[pltpu.VMEM((SEQ, LANES), F32)],
        compiler_params=pltpu.CompilerParams(vmem_limit_bytes=24 << 20),
        name="project_out",
    )(gathered, weights, activation)


CORES = [[0, 1], [2, 3]]


def body(tokens, embed, gain, w_in, short_filter, long_filter, skip_bias, w_out):
    core = lax.axis_index("pipe") % 2
    swap = [(0, 1), (1, 0), (2, 3), (3, 2)]

    own = jnp.concatenate(
        [
            short_filter[0].reshape(3 * STAPS, LANES),
            skip_bias,
            gain.astype(F32),
            jnp.zeros((1, LANES), F32),
            long_filter[0],
        ],
        axis=0,
    )
    other = hop(own, swap)
    first, second = jnp.where(core == 0, own, other), jnp.where(core == 0, other, own)
    w_in_both = lax.all_gather(w_in[0], "pipe", axis_index_groups=CORES)
    w_out_both = lax.all_gather(w_out[0], "pipe", axis_index_groups=CORES)
    w_in_both = w_in_both.reshape(2, 3, SIDE, SIDE, SIDE, LANES, LANES)
    w_out_both = w_out_both.reshape(2, SIDE, SIDE, SIDE, LANES, LANES)
    rows = 3 * STAPS + 3
    taps = [first[:rows], second[:rows]]
    toep = toeplitz(jnp.concatenate([first[rows:], second[rows:]], axis=0))
    toep = toep.reshape(2, LANES // GROUP, SEQ, TABLE)

    ids = lax.dynamic_index_in_dim(tokens, core, 0, keepdims=False)
    one_hot = (ids[:, None] == jnp.arange(embed.shape[0], dtype=jnp.int32)[None, :]).astype(BF16)
    activation = jnp.dot(one_hot, embed, preferred_element_type=F32).astype(BF16)

    gain_rows = jnp.concatenate(
        [first[rows - 2 : rows - 1], second[rows - 2 : rows - 1], jnp.zeros((EXTRA - 2, LANES), F32)],
        axis=0,
    )
    arrived = gather_channels(jnp.concatenate([activation, gain_rows.astype(BF16)], axis=0))
    gathered, gains = arrived[:, :, :SEQ], arrived[:, :, SEQ:]
    for part in range(2):
        for layer in range(2):
            if part + layer > 0:
                gathered = gather_channels(activation)
            gated = mix(layer, gathered, gains, w_in_both, taps[layer], toep)
            activation = project_out(layer, gather_channels(gated), w_out_both, activation)
        if part == 0:
            activation = hop(activation, [(0, 2), (1, 3)])

    quarters = activation.reshape(4, SEQ // 4, LANES)
    even, odd = quarters[0::2], quarters[1::2]
    keep = jnp.where(core == 0, even, odd)
    taken = hop(jnp.where(core == 0, odd, even), swap)
    row_0, row_1 = jnp.where(core == 0, keep, taken), jnp.where(core == 0, taken, keep)
    low, high = jnp.stack([row_0[0], row_1[0]]), jnp.stack([row_0[1], row_1[1]])
    passed = hop(low, [(2, 0), (3, 1)])
    return jnp.where(lax.axis_index("pipe") < 2, passed, high)


def solution(mesh):
    return jax.shard_map(
        body,
        mesh=mesh,
        in_specs=(
            P(),
            P(None, "fsdp"),
            P("pipe", "fsdp"),
            P("pipe", None, None, "fsdp"),
            P("pipe", None, None, "fsdp"),
            P("pipe", "fsdp", None),
            P("pipe", "fsdp"),
            P("pipe", None, "fsdp"),
        ),
        out_specs=P(None, "pipe", "fsdp"),
        check_vma=False,
    )
```

time: 2050 us -> 456 us (0.22)
  blocking collectives: 832 us -> 228 us
  waiting for transfers between devices: 592 us -> 92.7 us
  local copies, waits for them, and re-layouts: 502 us -> 27.2 us
  matrix products: 61.6 us -> 0.24 us
  Pallas kernels: 0 us -> 47.6 us
  starting transfers between devices: 12.8 us -> 43 us
  other arithmetic: 26.4 us -> 1.53 us
    psum x5 -> x0, blocking collectives: 832 us -> none  [layer_step(): squares = lax.psum(jnp.sum(widened * widened, axis=1), 'fsdp')]
    all_gather x10 -> x2, waiting for transfers between devices: 550 us -> 0.04 us  [the longest x1 0.02 us: body(): w_in_both = lax.all_gather(w_in[0], 'pipe', axis_index_groups=CORES)]
    gather x10 -> x0, local copies, waits for them, and re-layouts: 470 us -> none  [long_mix(): kernels[:, lag_index]]
    all_to_all x0 -> x13, blocking collectives: none -> 228 us  [share(): return lax.all_to_all(copies, AXES, 0, 0, axis_index_groups=groups)]
    all_to_all x0 -> x3, waiting for transfers between devices: none -> 85.6 us  [share(): return lax.all_to_all(copies, AXES, 0, 0, axis_index_groups=groups)]
    dot_general x20 -> x1, matrix products: 61.6 us -> 0.24 us  [body(): jnp.dot(one_hot, embed, preferred_element_type=F32).astype(BF16)]
    pallas_call x0 -> x9, Pallas kernels: none -> 47.6 us  [the longest x4 25.8 us: mix(): pl.pallas_call(kernel, grid=(SIDE, SIDE), in_specs=[pl.BlockSpec((1, SIDE...]
    psum x1 -> x0, waiting for transfers between devices: 41.6 us -> none  [spread(): return lax.psum(jnp.where(mine, value, jnp.zeros_like(value)), axis)]
  transfers between devices with their start and end apart: 16 -> 9, of which waited for: 11 -> 7; matrix products, arithmetic and copies ran while one was open for 24% -> 2% of each run, Pallas kernels for 0% -> 2%
where the time goes in v1:
time: 456 us; the launch traced here: 454 us
  blocking collectives  228 us (50%)
  waiting for transfers between devices  92.7 us (20%)
  Pallas kernels  47.6 us (10%)
  starting transfers between devices  43 us (9%)
  local copies, waits for them, and re-layouts  27.2 us (6%)
  between operations  13.8 us (3%)
    all_to_all x13, blocking collectives, share(): return lax.all_to_all(copies, AXES, 0, 0, axis_index_groups=groups)  228 us
    all_to_all x3, waiting for transfers between devices, share(): return lax.all_to_all(copies, AXES, 0, 0, axis_index_groups=groups)  85.6 us
    pallas_call x4, Pallas kernels, mix(): pl.pallas_call(kernel, grid=(SIDE, SIDE), in_specs=[pl.BlockSpec((1, SIDE...  25.8 us
    ppermute x4, starting transfers between devices, hop(): return lax.ppermute(value, AXES, pairs)  24.9 us
    pallas_call x4, Pallas kernels, project_out(): pl.pallas_call(out_kernel, grid=(SIDE, SIDE), in_specs=[pl.BlockSpec((1,...  19.7 us
    all_to_all x3, starting transfers between devices, share(): return lax.all_to_all(copies, AXES, 0, 0, axis_index_groups=groups)  18.1 us
    unnamed x32, local copies, waits for them, and re-layouts  13.1 us
    broadcast_in_dim x16, local copies, waits for them, and re-layouts, share(): copies = jnp.broadcast_to(value[None], (count,) + value.shape)  9.25 us
  transfers between devices with their start and end apart: 9, of which 7 were waited for; matrix products, arithmetic and copies ran while one was open for 2% of the time, Pallas kernels for 2%

profile of v1, /device:TPU:1, one launch (start us, length us, event | category | flops | bytes accessed | tf_op | source)
XLA Modules:
  0.0 454.4 jit_solution(17607155635437238292)
XLA Ops:
  7.4 3.3 collective-permute-start
  11.7 14.1 %all_to_all.80 = bf16[4,176,128]{2,1,0:T(8,128)(2,1)S(1)} all-to-all(bf16[4,176,128]{2,1,0:T(8,128)(2,1)S(1)} %broadcast_in_dim.40), channel_id=1, replica_groups={{0,4,8,12},{1,5,9,13},{2,6,10,14},{3,7,11,15},{16,20,24,28},{17,21,25,2..., dimensions={0} | all-to-all | bytes 360448 | tf_op jit(solution)/shard_map/all_to_all | solution.py:47
  28.3 6.8 %all-to-all-start.1 = ((bf16[16,4,176,128]{3,2,1,0:T(8,128)(2,1)}), bf16[16,4,176,128]{3,2,1,0:T(8,128)(2,1)}, u32[]{:S(2)}, u32[]{:S(2)}) async-start(bf16[16,4,176,128]{3,2,1,0:T(8,128)(2,1)} %broadcast_in_dim.41), calls=%async_computation.1 | async-start | bytes 5767168 | tf_op jit(solution)/shard_map/all_to_all | solution.py:47
  38.9 29.2 %all-to-all-done.1 = bf16[16,4,176,128]{3,2,1,0:T(8,128)(2,1)} async-done(((bf16[16,4,176,128]{3,2,1,0:T(8,128)(2,1)}), bf16[16,4,176,128]{3,2,1,0:T(8,128)(2,1)}, u32[]{:S(2)}, u32[]{:S(2)}) %all-to-all-start.1) | async-done | bytes 2883616 | tf_op jit(solution)/shard_map/all_to_all | solution.py:47
  68.1 3.5 slice.68.refs_0_
  72.7 4.6 %copy-done.2 = bf16[2,3,8192,128]{3,2,1,0:T(8,128)(2,1)S(1)} copy-done((bf16[2,3,8192,128]{3,2,1,0:T(8,128)(2,1)S(1)}, bf16[2,3,8192,128]{3,2,1,0:T(8,128)(2,1)}, u32[]{:S(2)}) %copy-start.2) | copy-done | bytes 12582936
  79.0 5.2 %mix.4 = bf16[160,128]{1,0:T(8,128)(2,1)S(1)} custom-call(bf16[16,4,160,128]{3,2,1,0:T(8,128)(2,1)S(1)} %copy-done.7, bf16[16,4,16,128]{3,2,1,0:T(8,128)(2,1)S(1)} %slice.69.refs_1_, bf16[2,3,4,4,4,128,128]{6,5,4,3,2,1,0:T(8,128)(2,1)S(1)} %bitcast.7, f32[24,128]{1,0:T(8,128)S(1)} %slice.70.refs_3_, bf16[2,8,160,256]{3,2,1,0:T(8,128)(2,1)S(1)} %bitcast.17), custom_call_target="tpu_custom_call" | custom-call | tf_op jit(solution)/shard_map/mix/pallas_call | solution.py:129
  84.2 14.6 %all_to_all.81 = bf16[4,160,128]{2,1,0:T(8,128)(2,1)S(1)} all-to-all(bf16[4,160,128]{2,1,0:T(8,128)(2,1)S(1)} %broadcast_in_dim.43), channel_id=1, replica_groups={{0,4,8,12},{1,5,9,13},{2,6,10,14},{3,7,11,15},{16,20,24,28},{17,21,25,2..., dimensions={0} | all-to-all | bytes 327680 | tf_op jit(solution)/shard_map/all_to_all | solution.py:47
  100.9 4.4 all-to-all-start.3
  105.4 29.9 %all-to-all-done.3.g_ref = bf16[16,4,160,128]{3,2,1,0:T(8,128)(2,1)} async-done(((bf16[16,4,160,128]{3,2,1,0:T(8,128)(2,1)}), bf16[16,4,160,128]{3,2,1,0:T(8,128)(2,1)}, u32[]{:S(2)}, u32[]{:S(2)}) %all-to-all-start.3) | async-done | bytes 2621472 | tf_op jit(solution)/shard_map/all_to_all | solution.py:47
  137.5 9.3 %project_out.4.x_ref = bf16[160,128]{1,0:T(8,128)(2,1)S(1)} custom-call(bf16[16,4,160,128]{3,2,1,0:T(8,128)(2,1)} %all-to-all-done.3.g_ref, bf16[2,4,4,4,128,128]{5,4,3,2,1,0:T(8,128)(2,1)S(1)} %bitcast.13, bf16[160,128]{1,0:T(8,128)(2,1)S(1)} %convolution_convert_fusion.x_ref), custom_call_target="tpu_custom_call" | custom-call | tf_op jit(solution)/shard_map/project_out/pallas_call | solution.py:170
  146.8 9.8 %all_to_all.82 = bf16[4,160,128]{2,1,0:T(8,128)(2,1)S(1)} all-to-all(bf16[4,160,128]{2,1,0:T(8,128)(2,1)S(1)} %broadcast_in_dim.45), channel_id=1, replica_groups={{0,4,8,12},{1,5,9,13},{2,6,10,14},{3,7,11,15},{16,20,24,28},{17,21,25,2..., dimensions={0} | all-to-all | bytes 327680 | tf_op jit(solution)/shard_map/all_to_all | solution.py:47
  158.7 6.9 %all-to-all-start.5 = ((bf16[16,4,160,128]{3,2,1,0:T(8,128)(2,1)}), bf16[16,4,160,128]{3,2,1,0:T(8,128)(2,1)}, u32[]{:S(2)}, u32[]{:S(2)}) async-start(bf16[16,4,160,128]{3,2,1,0:T(8,128)(2,1)} %broadcast_in_dim.46), calls=%async_computation.5 | async-start | bytes 5242880 | tf_op jit(solution)/shard_map/all_to_all | solution.py:47
  165.6 26.5 %all-to-all-done.5.refs_0_ = bf16[16,4,160,128]{3,2,1,0:T(8,128)(2,1)} async-done(((bf16[16,4,160,128]{3,2,1,0:T(8,128)(2,1)}), bf16[16,4,160,128]{3,2,1,0:T(8,128)(2,1)}, u32[]{:S(2)}, u32[]{:S(2)}) %all-to-all-start.5) | async-done | bytes 2621472 | tf_op jit(solution)/shard_map/all_to_all | solution.py:47
  192.0 4.6 %copy-done.3 = bf16[2,3,8192,128]{3,2,1,0:T(8,128)(2,1)S(1)} copy-done((bf16[2,3,8192,128]{3,2,1,0:T(8,128)(2,1)S(1)}, bf16[2,3,8192,128]{3,2,1,0:T(8,128)(2,1)}, u32[]{:S(2)}) %copy-start.3) | copy-done | bytes 12582936
  196.6 10.3 %mix.5 = bf16[160,128]{1,0:T(8,128)(2,1)S(1)} custom-call(bf16[16,4,160,128]{3,2,1,0:T(8,128)(2,1)} %all-to-all-done.5.refs_0_, bf16[16,4,16,128]{3,2,1,0:T(8,128)(2,1)S(1)} %slice.69.refs_1_, bf16[2,3,4,4,4,128,128]{6,5,4,3,2,1,0:T(8,128)(2,1)S(1)} %bitcast.8, f32[24,128]{1,0:T(8,128)S(1)} %slice.75.refs_3_, bf16[2,8,160,256]{3,2,1,0:T(8,128)(2,1)S(1)} %bitcast.18), custom_call_target="tpu_custom_call" | custom-call | tf_op jit(solution)/shard_map/mix/pallas_call | solution.py:129
  207.0 10.1 %all_to_all.83 = bf16[4,160,128]{2,1,0:T(8,128)(2,1)S(1)} all-to-all(bf16[4,160,128]{2,1,0:T(8,128)(2,1)S(1)} %broadcast_in_dim.47), channel_id=1, replica_groups={{0,4,8,12},{1,5,9,13},{2,6,10,14},{3,7,11,15},{16,20,24,28},{17,21,25,2..., dimensions={0} | all-to-all | bytes 327680 | tf_op jit(solution)/shard_map/all_to_all | solution.py:47
  217.6 37.9 %all_to_all.84.g_ref = bf16[16,4,160,128]{3,2,1,0:T(8,128)(2,1)S(1)} all-to-all(bf16[16,4,160,128]{3,2,1,0:T(8,128)(2,1)S(1)} %broadcast_in_dim.48), channel_id=1, replica_groups={{0,1,2,3,16,17,18,19,32,33,34,35,48,49,50,51},{4,5,6,7,20,21,22,23,36,3..., dimensions={0} | all-to-all | bytes 5242880 | tf_op jit(solution)/shard_map/all_to_all | solution.py:47
  255.5 3.4 project_out.5
  262.5 11.2 %all_to_all.85 = bf16[4,160,128]{2,1,0:T(8,128)(2,1)S(1)} all-to-all(bf16[4,160,128]{2,1,0:T(8,128)(2,1)S(1)} %broadcast_in_dim.49), channel_id=1, replica_groups={{0,4,8,12},{1,5,9,13},{2,6,10,14},{3,7,11,15},{16,20,24,28},{17,21,25,2..., dimensions={0} | all-to-all | bytes 327680 | tf_op jit(solution)/shard_map/all_to_all | solution.py:47
  274.2 28.1 %all_to_all.86.refs_0_ = bf16[16,4,160,128]{3,2,1,0:T(8,128)(2,1)S(1)} all-to-all(bf16[16,4,160,128]{3,2,1,0:T(8,128)(2,1)S(1)} %broadcast_in_dim.50), channel_id=1, replica_groups={{0,1,2,3,16,17,18,19,32,33,34,35,48,49,50,51},{4,5,6,7,20,21,22,23,36,3..., dimensions={0} | all-to-all | bytes 5242880 | tf_op jit(solution)/shard_map/all_to_all | solution.py:47
  302.3 5.2 %mix.6 = bf16[160,128]{1,0:T(8,128)(2,1)S(1)} custom-call(bf16[16,4,160,128]{3,2,1,0:T(8,128)(2,1)S(1)} %all_to_all.86.refs_0_, bf16[16,4,16,128]{3,2,1,0:T(8,128)(2,1)S(1)} %slice.69.refs_1_, bf16[2,3,4,4,4,128,128]{6,5,4,3,2,1,0:T(8,128)(2,1)S(1)} %bitcast.11, f32[24,128]{1,0:T(8,128)S(1)} %slice.70.refs_3_, bf16[2,8,160,256]{3,2,1,0:T(8,128)(2,1)S(1)} %bitcast.19), custom_call_target="tpu_custom_call" | custom-call | tf_op jit(solution)/shard_map/mix/pallas_call | solution.py:129
  307.5 9.8 %all_to_all.87 = bf16[4,160,128]{2,1,0:T(8,128)(2,1)S(1)} all-to-all(bf16[4,160,128]{2,1,0:T(8,128)(2,1)S(1)} %broadcast_in_dim.51), channel_id=1, replica_groups={{0,4,8,12},{1,5,9,13},{2,6,10,14},{3,7,11,15},{16,20,24,28},{17,21,25,2..., dimensions={0} | all-to-all | bytes 327680 | tf_op jit(solution)/shard_map/all_to_all | solution.py:47
  317.8 25.2 %all_to_all.88.g_ref = bf16[16,4,160,128]{3,2,1,0:T(8,128)(2,1)S(1)} all-to-all(bf16[16,4,160,128]{3,2,1,0:T(8,128)(2,1)S(1)} %broadcast_in_dim.52), channel_id=1, replica_groups={{0,1,2,3,16,17,18,19,32,33,34,35,48,49,50,51},{4,5,6,7,20,21,22,23,36,3..., dimensions={0} | all-to-all | bytes 5242880 | tf_op jit(solution)/shard_map/all_to_all | solution.py:47
  343.0 3.5 project_out.6.x_ref
  346.5 11.1 %all_to_all.89 = bf16[4,160,128]{2,1,0:T(8,128)(2,1)S(1)} all-to-all(bf16[4,160,128]{2,1,0:T(8,128)(2,1)S(1)} %broadcast_in_dim.53), channel_id=1, replica_groups={{0,4,8,12},{1,5,9,13},{2,6,10,14},{3,7,11,15},{16,20,24,28},{17,21,25,2..., dimensions={0} | all-to-all | bytes 327680 | tf_op jit(solution)/shard_map/all_to_all | solution.py:47
  358.1 22.8 %all_to_all.90.refs_0_ = bf16[16,4,160,128]{3,2,1,0:T(8,128)(2,1)S(1)} all-to-all(bf16[16,4,160,128]{3,2,1,0:T(8,128)(2,1)S(1)} %broadcast_in_dim.54), channel_id=1, replica_groups={{0,1,2,3,16,17,18,19,32,33,34,35,48,49,50,51},{4,5,6,7,20,21,22,23,36,3..., dimensions={0} | all-to-all | bytes 5242880 | tf_op jit(solution)/shard_map/all_to_all | solution.py:47
  380.9 5.2 %mix.7 = bf16[160,128]{1,0:T(8,128)(2,1)S(1)} custom-call(bf16[16,4,160,128]{3,2,1,0:T(8,128)(2,1)S(1)} %all_to_all.90.refs_0_, bf16[16,4,16,128]{3,2,1,0:T(8,128)(2,1)S(1)} %slice.69.refs_1_, bf16[2,3,4,4,4,128,128]{6,5,4,3,2,1,0:T(8,128)(2,1)S(1)} %bitcast.12, f32[24,128]{1,0:T(8,128)S(1)} %slice.75.refs_3_, bf16[2,8,160,256]{3,2,1,0:T(8,128)(2,1)S(1)} %bitcast.20), custom_call_target="tpu_custom_call" | custom-call | tf_op jit(solution)/shard_map/mix/pallas_call | solution.py:129
  386.1 9.8 %all_to_all.91 = bf16[4,160,128]{2,1,0:T(8,128)(2,1)S(1)} all-to-all(bf16[4,160,128]{2,1,0:T(8,128)(2,1)S(1)} %broadcast_in_dim.55), channel_id=1, replica_groups={{0,4,8,12},{1,5,9,13},{2,6,10,14},{3,7,11,15},{16,20,24,28},{17,21,25,2..., dimensions={0} | all-to-all | bytes 327680 | tf_op jit(solution)/shard_map/all_to_all | solution.py:47
  396.4 23.9 %all_to_all.92.g_ref = bf16[16,4,160,128]{3,2,1,0:T(8,128)(2,1)S(1)} all-to-all(bf16[16,4,160,128]{3,2,1,0:T(8,128)(2,1)S(1)} %broadcast_in_dim.56), channel_id=1, replica_groups={{0,1,2,3,16,17,18,19,32,33,34,35,48,49,50,51},{4,5,6,7,20,21,22,23,36,3..., dimensions={0} | all-to-all | bytes 5242880 | tf_op jit(solution)/shard_map/all_to_all | solution.py:47
  420.3 3.5 project_out.7
  423.8 17.8 %collective-permute-start.2 = (bf16[2,40,128]{2,1,0:T(8,128)(2,1)S(1)}, bf16[2,40,128]{2,1,0:T(8,128)(2,1)S(1)}, u32[]{:S(2)}, u32[]{:S(2)}) collective-permute-start(bf16[2,40,128]{2,1,0:T(8,128)(2,1)S(1)} %broadcast_select_fusion.2), channel_id=1, source_target_pairs={{0,64},{1,65},{2,66},{3,67},{4,68},{5,69},{6,70},{7,71},{8,72},{9,... | collective-permute-start | bytes 61448 | tf_op jit(solution)/shard_map/ppermute | solution.py:41
  (88 shorter events, 29.3 us)
Async XLA Ops:
  6.5 4.2 copy-start
  6.5 66.1 %all-gather.3.cloned.1.call-start = ((), (), s32[]{:S(2)}) async-start(), calls=%async_computation.16 | async-start | bytes 18874368 | tf_op jit(solution)/shard_map/all_gather | solution.py:205
  6.5 0.7 copy-start.8
  6.5 0.8 copy-start.9
  6.5 0.8 copy-start.10
  6.6 0.8 copy-start.11
  6.6 4.2 copy-start.12
  7.4 4.2 collective-permute-start
  28.3 39.9 %all-to-all-start.1 = ((bf16[16,4,176,128]{3,2,1,0:T(8,128)(2,1)}), bf16[16,4,176,128]{3,2,1,0:T(8,128)(2,1)}, u32[]{:S(2)}, u32[]{:S(2)}) async-start(bf16[16,4,176,128]{3,2,1,0:T(8,128)(2,1)} %broadcast_in_dim.41), calls=%async_computation.1 | async-start | bytes 5767168 | tf_op jit(solution)/shard_map/all_to_all | solution.py:47
  35.1 70.3 %all-gather.5.cloned.1.call-start = ((), (), s32[]{:S(2)}) async-start(), calls=%async_computation.17 | async-start | bytes 6291456 | tf_op jit(solution)/shard_map/all_gather | solution.py:206
  38.9 33.8 %copy-start.6 = (bf16[16,160,256]{2,1,0:T(8,128)(2,1)S(1)}, bf16[16,160,256]{2,1,0:T(8,128)(2,1)}, u32[]{:S(2)}) copy-start(bf16[16,160,256]{2,1,0:T(8,128)(2,1)} %toeplitz.1) | copy-start | bytes 3932164
  72.7 4.6 %copy-start.2 = (bf16[2,3,8192,128]{3,2,1,0:T(8,128)(2,1)S(1)}, bf16[2,3,8192,128]{3,2,1,0:T(8,128)(2,1)}, u32[]{:S(2)}) copy-start(bf16[2,3,8192,128]{3,2,1,0:T(8,128)(2,1)} %all-gather.3.cloned.1.call-done) | copy-start | bytes 37748740
  77.3 1.7 copy-start.7
  100.9 34.4 %all-to-all-start.3 = ((bf16[16,4,160,128]{3,2,1,0:T(8,128)(2,1)}), bf16[16,4,160,128]{3,2,1,0:T(8,128)(2,1)}, u32[]{:S(2)}, u32[]{:S(2)}) async-start(bf16[16,4,160,128]{3,2,1,0:T(8,128)(2,1)} %broadcast_in_dim.44), calls=%async_computation.3 | async-start | bytes 5242880 | tf_op jit(solution)/shard_map/all_to_all | solution.py:47
  135.3 2.2 copy-start.4
  158.7 33.4 %all-to-all-start.5 = ((bf16[16,4,160,128]{3,2,1,0:T(8,128)(2,1)}), bf16[16,4,160,128]{3,2,1,0:T(8,128)(2,1)}, u32[]{:S(2)}, u32[]{:S(2)}) async-start(bf16[16,4,160,128]{3,2,1,0:T(8,128)(2,1)} %broadcast_in_dim.46), calls=%async_computation.5 | async-start | bytes 5242880 | tf_op jit(solution)/shard_map/all_to_all | solution.py:47
  192.0 4.6 %copy-start.3 = (bf16[2,3,8192,128]{3,2,1,0:T(8,128)(2,1)S(1)}, bf16[2,3,8192,128]{3,2,1,0:T(8,128)(2,1)}, u32[]{:S(2)}) copy-start(bf16[2,3,8192,128]{3,2,1,0:T(8,128)(2,1)} %all-gather.3.cloned.1.call-done) | copy-start | bytes 37748740
  207.0 48.5 %copy-start.5 = (bf16[2,8192,128]{2,1,0:T(8,128)(2,1)S(1)}, bf16[2,8192,128]{2,1,0:T(8,128)(2,1)}, u32[]{:S(2)}) copy-start(bf16[2,8192,128]{2,1,0:T(8,128)(2,1)} %all-gather.5.cloned.1.call-done) | copy-start | bytes 12582916
  217.1 85.2 %slice-start = ((s8[12582912]{0:T(1024)(128)(4,1)}), s8[4194304]{0:T(1024)(128)(4,1)S(1)}, s32[]{:S(2)}) async-start(s8[12582912]{0:T(1024)(128)(4,1)} %bitcast.9), calls=%async_computation.18 | async-start | bytes 8388608
  217.6 84.7 %slice-start.1 = ((s8[12582912]{0:T(1024)(128)(4,1)}), s8[4194304]{0:T(1024)(128)(4,1)S(1)}, s32[]{:S(2)}) async-start(s8[12582912]{0:T(1024)(128)(4,1)} %bitcast.9), calls=%async_computation.19 | async-start | bytes 8388608
  258.9 3.6 collective-permute-start.1
  273.7 28.6 %slice-start.2 = ((s8[12582912]{0:T(1024)(128)(4,1)}), s8[4194304]{0:T(1024)(128)(4,1)S(1)}, s32[]{:S(2)}) async-start(s8[12582912]{0:T(1024)(128)(4,1)} %bitcast.9), calls=%async_computation.20 | async-start | bytes 8388608
  396.4 51.2 %copy-start.1 = (bf16[512,128]{1,0:T(8,128)(2,1)S(1)}, bf16[512,128]{1,0:T(8,128)(2,1)}, u32[]{:S(2)}) copy-start(bf16[512,128]{1,0:T(8,128)(2,1)} %param.9) | copy-start | bytes 393220
  423.8 18.6 %collective-permute-start.2 = (bf16[2,40,128]{2,1,0:T(8,128)(2,1)S(1)}, bf16[2,40,128]{2,1,0:T(8,128)(2,1)S(1)}, u32[]{:S(2)}, u32[]{:S(2)}) collective-permute-start(bf16[2,40,128]{2,1,0:T(8,128)(2,1)S(1)} %broadcast_select_fusion.2), channel_id=1, source_target_pairs={{0,64},{1,65},{2,66},{3,67},{4,68},{5,69},{6,70},{7,71},{8,72},{9,... | collective-permute-start | bytes 61448 | tf_op jit(solution)/shard_map/ppermute | solution.py:41
  442.5 4.5 collective-permute-start.3
Sparse Core Ops, SparseCore 0:
  9.2 34.7 all-gather.2
  45.8 20.2 all-gather.4

commit v2 on v1

--- a/solution.py
+++ b/solution.py
@@ -18,6 +18,7 @@
 PIPES = 4
 FSDP = 64
 EXTRA = 16
+VMEM_LIMIT = 48 << 20
 F32 = jnp.float32
 BF16 = jnp.bfloat16
 
@@ -72,113 +73,109 @@
     )(base)
 
 
-def mix_kernel(layer, x_ref, gain_ref, w_ref, taps_ref, toep_ref, out_ref, total, squares, padded):
-    step = pl.program_id(0) * SIDE + pl.program_id(1)
-
-    @pl.when(step == 0)
-    def _():
-        total[...] = jnp.zeros_like(total)
-        squares[...] = jnp.zeros_like(squares)
-
-    scaled = []
-    power = squares[...]
-    for z in range(SIDE):
-        wide = x_ref[0, z].astype(F32)
-        power = power + wide * wide
-        gain = gain_ref[0, z].astype(F32)[layer : layer + 1, :]
-        scaled.append((wide * gain).astype(BF16))
-    squares[...] = power
-    left = jnp.concatenate(scaled, axis=1)
-    right = jnp.concatenate(
-        [w_ref[0, j, 0, :, 0].reshape(SIDE * LANES, LANES) for j in range(3)], axis=1
-    )
-    total[...] += jnp.dot(left, right, preferred_element_type=F32)
-
-    @pl.when(step == SIDE * SIDE - 1)
-    def _():
-        mean = jnp.sum(squares[...], axis=1, keepdims=True) / D
-        inverse = lax.rsqrt(mean + 1e-06)
-        mixed = []
-        for j in range(3):
-            projected = (total[:, j * LANES : (j + 1) * LANES] * inverse).astype(BF16)
-            padded[j, :EXTRA] = jnp.zeros((EXTRA, LANES), F32)
-            padded[j, EXTRA:] = projected.astype(F32)
-            running = jnp.zeros((SEQ, LANES), F32)
-            for i in range(STAPS):
-                tap = taps_ref[j * STAPS + i : j * STAPS + i + 1, :]
-                running = running + tap * padded[j, EXTRA - i : EXTRA - i + SEQ, :]
-            mixed.append(running)
-        product = mixed[1] * mixed[2]
-        carried = taps_ref[3 * STAPS : 3 * STAPS + 1, :] * product
-        lane = lax.broadcasted_iota(jnp.int32, (TABLE, LANES), 1)
-        tall = jnp.concatenate([product, jnp.zeros((TABLE - SEQ, LANES), F32)], axis=0)
-        for f in range(LANES // GROUP):
-            kept = jnp.where(lane // GROUP == f, tall, 0.0).astype(BF16)
-            carried = carried + jnp.dot(toep_ref[0, f], kept, preferred_element_type=F32)
-        out_ref[...] = (mixed[0] * carried).astype(BF16)
+def fetch(layer, weights_ref, held, sems):
+    copies = []
+    for x in range(SIDE):
+        source, target = weights_ref.at[layer, ..., x, :, :, :, :], held.at[..., x, :, :, :, :]
+        copies.append(pltpu.make_async_copy(source, target, sems.at[x]))
+    for copy in copies:
+        copy.start()
+    return copies
+
+
+def mix_kernel(layer, x_ref, gain_ref, w_ref, taps_ref, toep_ref, out_ref, held, sems, total, padded):
+    copies = fetch(layer, w_ref, held, sems)
+    power = jnp.zeros((SEQ, LANES), F32)
+    for x in range(SIDE):
+        scaled = []
+        for z in range(SIDE):
+            for y in range(SIDE):
+                wide = x_ref[x * SIDE + y, z, :SEQ].astype(F32)
+                power = power + wide * wide
+                gain = gain_ref[x * SIDE + y, z].astype(F32)[layer : layer + 1, :]
+                scaled.append((wide * gain).astype(BF16))
+        left = jnp.concatenate(scaled, axis=1)
+        copies[x].wait()
+        right = jnp.concatenate(
+            [held[j, x].reshape(SIDE * SIDE * LANES, LANES) for j in range(3)], axis=1
+        )
+        term = jnp.dot(left, right, preferred_element_type=F32)
+        total[...] = term if x == 0 else total[...] + term
+
+    mean = jnp.sum(power, axis=1, keepdims=True) / D
+    inverse = lax.rsqrt(mean + 1e-06)
+    mixed = []
+    for j in range(3):
+        projected = (total[:, j * LANES : (j + 1) * LANES] * inverse).astype(BF16)
+        padded[j, :EXTRA] = jnp.zeros((EXTRA, LANES), F32)
+        padded[j, EXTRA:] = projected.astype(F32)
+        running = jnp.zeros((SEQ, LANES), F32)
+        for i in range(STAPS):
+            tap = taps_ref[j * STAPS + i : j * STAPS + i + 1, :]
+            running = running + tap * padded[j, EXTRA - i : EXTRA - i + SEQ, :]
+        mixed.append(running)
+    product = mixed[1] * mixed[2]
+    carried = taps_ref[3 * STAPS : 3 * STAPS + 1, :] * product
+    lane = lax.broadcasted_iota(jnp.int32, (TABLE, LANES), 1)
+    tall = jnp.concatenate([product, jnp.zeros((TABLE - SEQ, LANES), F32)], axis=0)
+    for f in range(LANES // GROUP):
+        kept = jnp.where(lane // GROUP == f, tall, 0.0).astype(BF16)
+        carried = carried + jnp.dot(toep_ref[layer, f], kept, preferred_element_type=F32)
+    out_ref[...] = (mixed[0] * carried).astype(BF16)
+
+
+VMEM = pl.BlockSpec(memory_space=pltpu.VMEM)
+HBM = pl.BlockSpec(memory_space=pltpu.HBM)
 
 
 def mix(layer, gathered, gains, weights, taps, toep):
-    def whole(shape, first=0):
-        return pl.BlockSpec(shape, lambda x, y: (first,) + (0,) * (len(shape) - 1))
-
     def kernel(*refs):
         mix_kernel(layer, *refs)
 
-    filters = LANES // GROUP
     return pl.pallas_call(
         kernel,
-        grid=(SIDE, SIDE),
-        in_specs=[
-            pl.BlockSpec((1, SIDE, SEQ, LANES), lambda x, y: (x * SIDE + y, 0, 0, 0)),
-            pl.BlockSpec((1, SIDE, EXTRA, LANES), lambda x, y: (x * SIDE + y, 0, 0, 0)),
-            pl.BlockSpec(
-                (1, 3, 1, SIDE, 1, LANES, LANES), lambda x, y: (layer, 0, x, 0, y, 0, 0)
-            ),
-            whole((3 * STAPS + 3, LANES)),
-            whole((1, filters, SEQ, TABLE), layer),
-        ],
-        out_specs=whole((SEQ, LANES)),
+        in_specs=[VMEM, VMEM, HBM, VMEM, VMEM],
+        out_specs=VMEM,
         out_shape=jax.ShapeDtypeStruct((SEQ, LANES), BF16),
         scratch_shapes=[
+            pltpu.VMEM((3, SIDE, SIDE, SIDE, LANES, LANES), BF16),
+            pltpu.SemaphoreType.DMA((SIDE,)),
             pltpu.VMEM((SEQ, 3 * LANES), F32),
-            pltpu.VMEM((SEQ, LANES), F32),
             pltpu.VMEM((3, EXTRA + SEQ, LANES), F32),
         ],
-        compiler_params=pltpu.CompilerParams(vmem_limit_bytes=24 << 20),
+        compiler_params=pltpu.CompilerParams(vmem_limit_bytes=VMEM_LIMIT),
         name="mix",
     )(gathered, gains, weights, taps, toep)
 
 
-def out_kernel(g_ref, w_ref, x_ref, out_ref, total):
-    step = pl.program_id(0) * SIDE + pl.program_id(1)
-
-    @pl.when(step == 0)
-    def _():
-        total[...] = x_ref[...].astype(F32)
-
-    left = jnp.concatenate([g_ref[0, z] for z in range(SIDE)], axis=1)
-    right = w_ref[0, 0, :, 0].reshape(SIDE * LANES, LANES)
-    total[...] += jnp.dot(left, right, preferred_element_type=F32)
-
-    @pl.when(step == SIDE * SIDE - 1)
-    def _():
-        out_ref[...] = total[...].astype(BF16)
+def out_kernel(layer, g_ref, w_ref, x_ref, out_ref, held, sems, total):
+    copies = fetch(layer, w_ref, held, sems)
+    total[...] = x_ref[...].astype(F32)
+    for x in range(SIDE):
+        left = jnp.concatenate(
+            [g_ref[x * SIDE + y, z] for z in range(SIDE) for y in range(SIDE)], axis=1
+        )
+        copies[x].wait()
+        right = held[x].reshape(SIDE * SIDE * LANES, LANES)
+        total[...] += jnp.dot(left, right, preferred_element_type=F32)
+    out_ref[...] = total[...].astype(BF16)
 
 
 def project_out(layer, gathered, weights, activation):
+    def kernel(*refs):
+        out_kernel(layer, *refs)
+
     return pl.pallas_call(
-        out_kernel,
-        grid=(SIDE, SIDE),
-        in_specs=[
-            pl.BlockSpec((1, SIDE, SEQ, LANES), lambda x, y: (x * SIDE + y, 0, 0, 0)),
-            pl.BlockSpec((1, 1, SIDE, 1, LANES, LANES), lambda x, y: (layer, x, 0, y, 0, 0)),
-            pl.BlockSpec((SEQ, LANES), lambda x, y: (0, 0)),
+        kernel,
+        in_specs=[VMEM, HBM, VMEM],
+        out_specs=VMEM,
+        out_shape=jax.ShapeDtypeStruct((SEQ, LANES), BF16),
+        scratch_shapes=[
+            pltpu.VMEM((SIDE, SIDE, SIDE, LANES, LANES), BF16),
+            pltpu.SemaphoreType.DMA((SIDE,)),
+            pltpu.VMEM((SEQ, LANES), F32),
         ],
-        out_specs=pl.BlockSpec((SEQ, LANES), lambda x, y: (0, 0)),
-        out_shape=jax.ShapeDtypeStruct((SEQ, LANES), BF16),
-        scratch_shapes=[pltpu.VMEM((SEQ, LANES), F32)],
-        compiler_params=pltpu.CompilerParams(vmem_limit_bytes=24 << 20),
+        compiler_params=pltpu.CompilerParams(vmem_limit_bytes=VMEM_LIMIT),
         name="project_out",
     )(gathered, weights, activation)
 
@@ -220,7 +217,7 @@
         axis=0,
     )
     arrived = gather_channels(jnp.concatenate([activation, gain_rows.astype(BF16)], axis=0))
-    gathered, gains = arrived[:, :, :SEQ], arrived[:, :, SEQ:]
+    gathered, gains = arrived, arrived[:, :, SEQ:]
     for part in range(2):
         for layer in range(2):
             if part + layer > 0:

time: 456 us -> 423 us (0.928)
  Pallas kernels: 47.6 us -> 31.3 us
  local copies, waits for them, and re-layouts: 27.2 us -> 10.9 us
    pallas_call x8, Pallas kernels: 45.5 us -> 29.2 us  [the longest x4 19.2 us: mix(): pl.pallas_call(kernel, in_specs=[VMEM, VMEM, HBM, VMEM, VMEM], out_specs=...]
    unnamed x32 -> x18, local copies, waits for them, and re-layouts: 13.1 us -> 1.36 us
  transfers between devices with their start and end apart: 9 -> 9, of which waited for: 7 -> 7; matrix products, arithmetic and copies ran while one was open for 2% -> 1% of each run, Pallas kernels for 2% -> 2%
where the time goes in v2:
time: 423 us; the launch traced here: 422 us
  blocking collectives  231 us (55%)
  waiting for transfers between devices  92.7 us (22%)
  starting transfers between devices  41.1 us (10%)
  Pallas kernels  31.3 us (7%)
  between operations  13.8 us (3%)
  local copies, waits for them, and re-layouts  10.9 us (3%)
    all_to_all x13, blocking collectives, share(): return lax.all_to_all(copies, AXES, 0, 0, axis_index_groups=groups)  231 us
    all_to_all x3, waiting for transfers between devices, share(): return lax.all_to_all(copies, AXES, 0, 0, axis_index_groups=groups)  85.6 us
    ppermute x4, starting transfers between devices, hop(): return lax.ppermute(value, AXES, pairs)  23.9 us
    pallas_call x4, Pallas kernels, mix(): pl.pallas_call(kernel, in_specs=[VMEM, VMEM, HBM, VMEM, VMEM], out_specs=...  19.2 us
    all_to_all x3, starting transfers between devices, share(): return lax.all_to_all(copies, AXES, 0, 0, axis_index_groups=groups)  17.2 us
    pallas_call x4, Pallas kernels, project_out(): pl.pallas_call(kernel, in_specs=[VMEM, HBM, VMEM], out_specs=VMEM, out_sh...  9.97 us
    broadcast_in_dim x16, local copies, waits for them, and re-layouts, share(): copies = jnp.broadcast_to(value[None], (count,) + value.shape)  9.21 us
  transfers between devices with their start and end apart: 9, of which 7 were waited for; matrix products, arithmetic and copies ran while one was open for 1% of the time, Pallas kernels for 2%

profile of v2, /device:TPU:1, one launch (start us, length us, event | category | flops | bytes accessed | tf_op | source)
XLA Modules:
  0.0 422.3 jit_solution(18086113484274715749)
XLA Ops:
  7.4 3.3 collective-permute-start
  11.7 14.1 %all_to_all.80 = bf16[4,176,128]{2,1,0:T(8,128)(2,1)S(1)} all-to-all(bf16[4,176,128]{2,1,0:T(8,128)(2,1)S(1)} %broadcast_in_dim.40), channel_id=1, replica_groups={{0,4,8,12},{1,5,9,13},{2,6,10,14},{3,7,11,15},{16,20,24,28},{17,21,25,2..., dimensions={0} | all-to-all | bytes 360448 | tf_op jit(solution)/shard_map/all_to_all | solution.py:48
  25.8 2.5 broadcast_in_dim.41
  28.3 6.8 %all-to-all-start.1 = ((bf16[16,4,176,128]{3,2,1,0:T(8,128)(2,1)}), bf16[16,4,176,128]{3,2,1,0:T(8,128)(2,1)S(1)}, u32[]{:S(2)}, u32[]{:S(2)}) async-start(bf16[16,4,176,128]{3,2,1,0:T(8,128)(2,1)} %broadcast_in_dim.41), calls=%async_computation.1 | async-start | bytes 5767168 | tf_op jit(solution)/shard_map/all_to_all | solution.py:48
  38.9 29.2 %all-to-all-done.1.refs_0_ = bf16[16,4,176,128]{3,2,1,0:T(8,128)(2,1)S(1)} async-done(((bf16[16,4,176,128]{3,2,1,0:T(8,128)(2,1)}), bf16[16,4,176,128]{3,2,1,0:T(8,128)(2,1)S(1)}, u32[]{:S(2)}, u32[]{:S(2)}) %all-to-all-start.1) | async-done | bytes 2883616 | tf_op jit(solution)/shard_map/all_to_all | solution.py:48
  69.4 4.4 %mix.4 = bf16[160,128]{1,0:T(8,128)(2,1)S(1)} custom-call(bf16[16,4,176,128]{3,2,1,0:T(8,128)(2,1)S(1)} %all-to-all-done.1.refs_0_, bf16[16,4,16,128]{3,2,1,0:T(8,128)(2,1)S(1)} %slice.64.refs_1_, bf16[2,3,4,4,4,128,128]{6,5,4,3,2,1,0:T(8,128)(2,1)} %bitcast.13, f32[24,128]{1,0:T(8,128)S(1)} %slice.65.refs_3_, bf16[2,8,160,256]{3,2,1,0:T(8,128)(2,1)S(1)} %bitcast.7), custom_call_target="tpu_custom_call" | custom-call | tf_op jit(solution)/shard_map/mix/pallas_call | solution.py:135
  73.8 14.6 %all_to_all.81 = bf16[4,160,128]{2,1,0:T(8,128)(2,1)S(1)} all-to-all(bf16[4,160,128]{2,1,0:T(8,128)(2,1)S(1)} %broadcast_in_dim.43), channel_id=1, replica_groups={{0,4,8,12},{1,5,9,13},{2,6,10,14},{3,7,11,15},{16,20,24,28},{17,21,25,2..., dimensions={0} | all-to-all | bytes 327680 | tf_op jit(solution)/shard_map/all_to_all | solution.py:48
  90.5 3.7 all-to-all-start.3
  94.2 29.9 %all-to-all-done.3.refs_0_ = bf16[16,4,160,128]{3,2,1,0:T(8,128)(2,1)S(1)} async-done(((bf16[16,4,160,128]{3,2,1,0:T(8,128)(2,1)}), bf16[16,4,160,128]{3,2,1,0:T(8,128)(2,1)S(1)}, u32[]{:S(2)}, u32[]{:S(2)}) %all-to-all-start.3) | async-done | bytes 2621472 | tf_op jit(solution)/shard_map/all_to_all | solution.py:48
  124.1 2.5 project_out.4.refs_2_
  126.7 10.4 %all_to_all.82 = bf16[4,160,128]{2,1,0:T(8,128)(2,1)S(1)} all-to-all(bf16[4,160,128]{2,1,0:T(8,128)(2,1)S(1)} %broadcast_in_dim.45), channel_id=1, replica_groups={{0,4,8,12},{1,5,9,13},{2,6,10,14},{3,7,11,15},{16,20,24,28},{17,21,25,2..., dimensions={0} | all-to-all | bytes 327680 | tf_op jit(solution)/shard_map/all_to_all | solution.py:48
  139.1 6.8 %all-to-all-start.5 = ((bf16[16,4,160,128]{3,2,1,0:T(8,128)(2,1)}), bf16[16,4,160,128]{3,2,1,0:T(8,128)(2,1)}, u32[]{:S(2)}, u32[]{:S(2)}) async-start(bf16[16,4,160,128]{3,2,1,0:T(8,128)(2,1)} %broadcast_in_dim.46), calls=%async_computation.5 | async-start | bytes 5242880 | tf_op jit(solution)/shard_map/all_to_all | solution.py:48
  145.9 26.5 %all-to-all-done.5.refs_0_ = bf16[16,4,160,128]{3,2,1,0:T(8,128)(2,1)} async-done(((bf16[16,4,160,128]{3,2,1,0:T(8,128)(2,1)}), bf16[16,4,160,128]{3,2,1,0:T(8,128)(2,1)}, u32[]{:S(2)}, u32[]{:S(2)}) %all-to-all-start.5) | async-done | bytes 2621472 | tf_op jit(solution)/shard_map/all_to_all | solution.py:48
  172.4 6.1 %mix.5 = bf16[160,128]{1,0:T(8,128)(2,1)S(1)} custom-call(bf16[16,4,160,128]{3,2,1,0:T(8,128)(2,1)} %all-to-all-done.5.refs_0_, bf16[16,4,16,128]{3,2,1,0:T(8,128)(2,1)S(1)} %slice.64.refs_1_, bf16[2,3,4,4,4,128,128]{6,5,4,3,2,1,0:T(8,128)(2,1)} %bitcast.14, f32[24,128]{1,0:T(8,128)S(1)} %slice.70.refs_3_, bf16[2,8,160,256]{3,2,1,0:T(8,128)(2,1)S(1)} %bitcast.8), custom_call_target="tpu_custom_call" | custom-call | tf_op jit(solution)/shard_map/mix/pallas_call | solution.py:135
  178.5 9.8 %all_to_all.83 = bf16[4,160,128]{2,1,0:T(8,128)(2,1)S(1)} all-to-all(bf16[4,160,128]{2,1,0:T(8,128)(2,1)S(1)} %broadcast_in_dim.47), channel_id=1, replica_groups={{0,4,8,12},{1,5,9,13},{2,6,10,14},{3,7,11,15},{16,20,24,28},{17,21,25,2..., dimensions={0} | all-to-all | bytes 327680 | tf_op jit(solution)/shard_map/all_to_all | solution.py:48
  188.8 35.7 %all_to_all.84.refs_0_ = bf16[16,4,160,128]{3,2,1,0:T(8,128)(2,1)S(1)} all-to-all(bf16[16,4,160,128]{3,2,1,0:T(8,128)(2,1)S(1)} %broadcast_in_dim.48), channel_id=1, replica_groups={{0,1,2,3,16,17,18,19,32,33,34,35,48,49,50,51},{4,5,6,7,20,21,22,23,36,3..., dimensions={0} | all-to-all | bytes 5242880 | tf_op jit(solution)/shard_map/all_to_all | solution.py:48
  224.5 2.5 project_out.5
  227.0 2.6 collective-permute-start.1
  230.8 12.8 %all_to_all.85 = bf16[4,160,128]{2,1,0:T(8,128)(2,1)S(1)} all-to-all(bf16[4,160,128]{2,1,0:T(8,128)(2,1)S(1)} %broadcast_in_dim.49), channel_id=1, replica_groups={{0,4,8,12},{1,5,9,13},{2,6,10,14},{3,7,11,15},{16,20,24,28},{17,21,25,2..., dimensions={0} | all-to-all | bytes 327680 | tf_op jit(solution)/shard_map/all_to_all | solution.py:48
  244.1 28.8 %all_to_all.86.refs_0_ = bf16[16,4,160,128]{3,2,1,0:T(8,128)(2,1)S(1)} all-to-all(bf16[16,4,160,128]{3,2,1,0:T(8,128)(2,1)S(1)} %broadcast_in_dim.50), channel_id=1, replica_groups={{0,1,2,3,16,17,18,19,32,33,34,35,48,49,50,51},{4,5,6,7,20,21,22,23,36,3..., dimensions={0} | all-to-all | bytes 5242880 | tf_op jit(solution)/shard_map/all_to_all | solution.py:48
  272.8 4.4 %mix.6 = bf16[160,128]{1,0:T(8,128)(2,1)S(1)} custom-call(bf16[16,4,160,128]{3,2,1,0:T(8,128)(2,1)S(1)} %all_to_all.86.refs_0_, bf16[16,4,16,128]{3,2,1,0:T(8,128)(2,1)S(1)} %slice.64.refs_1_, bf16[2,3,4,4,4,128,128]{6,5,4,3,2,1,0:T(8,128)(2,1)} %bitcast.15, f32[24,128]{1,0:T(8,128)S(1)} %slice.65.refs_3_, bf16[2,8,160,256]{3,2,1,0:T(8,128)(2,1)S(1)} %bitcast.9), custom_call_target="tpu_custom_call" | custom-call | tf_op jit(solution)/shard_map/mix/pallas_call | solution.py:135
  277.2 9.8 %all_to_all.87 = bf16[4,160,128]{2,1,0:T(8,128)(2,1)S(1)} all-to-all(bf16[4,160,128]{2,1,0:T(8,128)(2,1)S(1)} %broadcast_in_dim.51), channel_id=1, replica_groups={{0,4,8,12},{1,5,9,13},{2,6,10,14},{3,7,11,15},{16,20,24,28},{17,21,25,2..., dimensions={0} | all-to-all | bytes 327680 | tf_op jit(solution)/shard_map/all_to_all | solution.py:48
  287.5 25.4 %all_to_all.88.refs_0_ = bf16[16,4,160,128]{3,2,1,0:T(8,128)(2,1)S(1)} all-to-all(bf16[16,4,160,128]{3,2,1,0:T(8,128)(2,1)S(1)} %broadcast_in_dim.52), channel_id=1, replica_groups={{0,1,2,3,16,17,18,19,32,33,34,35,48,49,50,51},{4,5,6,7,20,21,22,23,36,3..., dimensions={0} | all-to-all | bytes 5242880 | tf_op jit(solution)/shard_map/all_to_all | solution.py:48
  312.9 2.5 project_out.6.refs_2_
  315.5 11.3 %all_to_all.89 = bf16[4,160,128]{2,1,0:T(8,128)(2,1)S(1)} all-to-all(bf16[4,160,128]{2,1,0:T(8,128)(2,1)S(1)} %broadcast_in_dim.53), channel_id=1, replica_groups={{0,4,8,12},{1,5,9,13},{2,6,10,14},{3,7,11,15},{16,20,24,28},{17,21,25,2..., dimensions={0} | all-to-all | bytes 327680 | tf_op jit(solution)/shard_map/all_to_all | solution.py:48
  327.3 23.9 %all_to_all.90.refs_0_ = bf16[16,4,160,128]{3,2,1,0:T(8,128)(2,1)S(1)} all-to-all(bf16[16,4,160,128]{3,2,1,0:T(8,128)(2,1)S(1)} %broadcast_in_dim.54), channel_id=1, replica_groups={{0,1,2,3,16,17,18,19,32,33,34,35,48,49,50,51},{4,5,6,7,20,21,22,23,36,3..., dimensions={0} | all-to-all | bytes 5242880 | tf_op jit(solution)/shard_map/all_to_all | solution.py:48
  351.2 4.4 %mix.7 = bf16[160,128]{1,0:T(8,128)(2,1)S(1)} custom-call(bf16[16,4,160,128]{3,2,1,0:T(8,128)(2,1)S(1)} %all_to_all.90.refs_0_, bf16[16,4,16,128]{3,2,1,0:T(8,128)(2,1)S(1)} %slice.64.refs_1_, bf16[2,3,4,4,4,128,128]{6,5,4,3,2,1,0:T(8,128)(2,1)} %bitcast.16, f32[24,128]{1,0:T(8,128)S(1)} %slice.70.refs_3_, bf16[2,8,160,256]{3,2,1,0:T(8,128)(2,1)S(1)} %bitcast.10), custom_call_target="tpu_custom_call" | custom-call | tf_op jit(solution)/shard_map/mix/pallas_call | solution.py:135
  355.6 10.6 %all_to_all.91 = bf16[4,160,128]{2,1,0:T(8,128)(2,1)S(1)} all-to-all(bf16[4,160,128]{2,1,0:T(8,128)(2,1)S(1)} %broadcast_in_dim.55), channel_id=1, replica_groups={{0,4,8,12},{1,5,9,13},{2,6,10,14},{3,7,11,15},{16,20,24,28},{17,21,25,2..., dimensions={0} | all-to-all | bytes 327680 | tf_op jit(solution)/shard_map/all_to_all | solution.py:48
  366.8 23.6 %all_to_all.92.refs_0_ = bf16[16,4,160,128]{3,2,1,0:T(8,128)(2,1)S(1)} all-to-all(bf16[16,4,160,128]{3,2,1,0:T(8,128)(2,1)S(1)} %broadcast_in_dim.56), channel_id=1, replica_groups={{0,1,2,3,16,17,18,19,32,33,34,35,48,49,50,51},{4,5,6,7,20,21,22,23,36,3..., dimensions={0} | all-to-all | bytes 5242880 | tf_op jit(solution)/shard_map/all_to_all | solution.py:48
  390.4 2.5 project_out.7
  392.9 16.6 %collective-permute-start.2 = (bf16[2,40,128]{2,1,0:T(8,128)(2,1)S(1)}, bf16[2,40,128]{2,1,0:T(8,128)(2,1)S(1)}, u32[]{:S(2)}, u32[]{:S(2)}) collective-permute-start(bf16[2,40,128]{2,1,0:T(8,128)(2,1)S(1)} %broadcast_select_fusion.2), channel_id=1, source_target_pairs={{0,64},{1,65},{2,66},{3,67},{4,68},{5,69},{6,70},{7,71},{8,72},{9,... | collective-permute-start | bytes 61448 | tf_op jit(solution)/shard_map/ppermute | solution.py:42
  411.7 3.2 collective-permute-done.3
  (72 shorter events, 17.5 us)
Async XLA Ops:
  6.5 4.2 copy-start
  6.5 61.5 %all-gather.3.cloned.1.call-start = ((), (), s32[]{:S(2)}) async-start(), calls=%async_computation.16 | async-start | bytes 18874368 | tf_op jit(solution)/shard_map/all_gather | solution.py:202
  6.5 0.7 copy-start.4
  6.5 0.8 copy-start.5
  6.5 0.8 copy-start.6
  6.6 0.8 copy-start.7
  6.6 4.2 copy-start.8
  7.4 4.2 collective-permute-start
  28.3 39.7 %all-to-all-start.1 = ((bf16[16,4,176,128]{3,2,1,0:T(8,128)(2,1)}), bf16[16,4,176,128]{3,2,1,0:T(8,128)(2,1)S(1)}, u32[]{:S(2)}, u32[]{:S(2)}) async-start(bf16[16,4,176,128]{3,2,1,0:T(8,128)(2,1)} %broadcast_in_dim.41), calls=%async_computation.1 | async-start | bytes 5767168 | tf_op jit(solution)/shard_map/all_to_all | solution.py:48
  35.1 59.2 %all-gather.5.cloned.1.call-start = ((), (), s32[]{:S(2)}) async-start(), calls=%async_computation.17 | async-start | bytes 6291456 | tf_op jit(solution)/shard_map/all_gather | solution.py:203
  68.1 1.3 copy-start.2
  90.5 33.7 %all-to-all-start.3 = ((bf16[16,4,160,128]{3,2,1,0:T(8,128)(2,1)}), bf16[16,4,160,128]{3,2,1,0:T(8,128)(2,1)S(1)}, u32[]{:S(2)}, u32[]{:S(2)}) async-start(bf16[16,4,160,128]{3,2,1,0:T(8,128)(2,1)} %broadcast_in_dim.44), calls=%async_computation.3 | async-start | bytes 5242880 | tf_op jit(solution)/shard_map/all_to_all | solution.py:48
  139.1 33.3 %copy-start.3 = (bf16[16,160,256]{2,1,0:T(8,128)(2,1)S(1)}, bf16[16,160,256]{2,1,0:T(8,128)(2,1)}, u32[]{:S(2)}) copy-start(bf16[16,160,256]{2,1,0:T(8,128)(2,1)} %toeplitz.1) | copy-start | bytes 3932164
  139.1 33.3 %all-to-all-start.5 = ((bf16[16,4,160,128]{3,2,1,0:T(8,128)(2,1)}), bf16[16,4,160,128]{3,2,1,0:T(8,128)(2,1)}, u32[]{:S(2)}, u32[]{:S(2)}) async-start(bf16[16,4,160,128]{3,2,1,0:T(8,128)(2,1)} %broadcast_in_dim.46), calls=%async_computation.5 | async-start | bytes 5242880 | tf_op jit(solution)/shard_map/all_to_all | solution.py:48
  227.0 3.7 collective-permute-start.1
  366.7 48.8 %copy-start.1 = (bf16[512,128]{1,0:T(8,128)(2,1)S(1)}, bf16[512,128]{1,0:T(8,128)(2,1)}, u32[]{:S(2)}) copy-start(bf16[512,128]{1,0:T(8,128)(2,1)} %param.9) | copy-start | bytes 393220
  392.9 17.4 %collective-permute-start.2 = (bf16[2,40,128]{2,1,0:T(8,128)(2,1)S(1)}, bf16[2,40,128]{2,1,0:T(8,128)(2,1)S(1)}, u32[]{:S(2)}, u32[]{:S(2)}) collective-permute-start(bf16[2,40,128]{2,1,0:T(8,128)(2,1)S(1)} %broadcast_select_fusion.2), channel_id=1, source_target_pairs={{0,64},{1,65},{2,66},{3,67},{4,68},{5,69},{6,70},{7,71},{8,72},{9,... | collective-permute-start | bytes 61448 | tf_op jit(solution)/shard_map/ppermute | solution.py:42
  410.4 4.5 %collective-permute-start.3 = (bf16[2,40,128]{2,1,0:T(8,128)(2,1)S(1)}, bf16[2,40,128]{2,1,0:T(8,128)(2,1)S(1)}, u32[]{:S(2)}, u32[]{:S(2)}) collective-permute-start(bf16[2,40,128]{2,1,0:T(8,128)(2,1)S(1)} %pad_maximum_fusion), channel_id=1, source_target_pairs={{128,0},{129,1},{130,2},{131,3},{132,4},{133,5},{134,6},{135,7},{1... | collective-permute-start | bytes 61448 | tf_op jit(solution)/shard_map/ppermute | solution.py:42
Sparse Core Ops, SparseCore 0:
  9.2 34.7 all-gather.2
  45.8 20.2 all-gather.4

commit v3 on v2

--- a/solution.py
+++ b/solution.py
@@ -50,6 +50,15 @@
 
 def gather_channels(block):
     return share(share(block, LINES_Z), PLANES_XY)
+
+
+def gather_in_turn(block, core):
+    copies = jnp.broadcast_to(block[None], (SIDE,) + block.shape)
+    ahead = lax.cond(core == 1, lambda b: share(b, LINES_Z), lambda b: copies, block)
+    turn = hop(ahead[0, :EXTRA], [(1, 0), (3, 2)])
+    block = jnp.concatenate([block[: SEQ + 2], turn[2:]], axis=0)
+    line = lax.cond(core == 0, lambda b, a: share(b, LINES_Z), lambda b, a: a, block, ahead)
+    return share(line, PLANES_XY)
 
 
 def toeplitz_kernel(base_ref, out_ref):
@@ -216,7 +225,9 @@
         [first[rows - 2 : rows - 1], second[rows - 2 : rows - 1], jnp.zeros((EXTRA - 2, LANES), F32)],
         axis=0,
     )
-    arrived = gather_channels(jnp.concatenate([activation, gain_rows.astype(BF16)], axis=0))
+    arrived = gather_in_turn(
+        jnp.concatenate([activation, gain_rows.astype(BF16)], axis=0), core
+    )
     gathered, gains = arrived, arrived[:, :, SEQ:]
     for part in range(2):
         for layer in range(2):

time: 423 us -> 423 us (level)
  starting transfers between devices: 41.1 us -> 57 us
  waiting for transfers between devices: 92.7 us -> 80.5 us
  blocking collectives: 231 us -> 226 us
    all_to_all x3, starting transfers between devices: 17.2 us -> 31.6 us  [share(): return lax.all_to_all(copies, AXES, 0, 0, axis_index_groups=groups)]
    all_to_all x3, waiting for transfers between devices: 85.6 us -> 72.6 us  [share(): return lax.all_to_all(copies, AXES, 0, 0, axis_index_groups=groups)]
    all_to_all x13, blocking collectives: 231 us -> 226 us  [share(): return lax.all_to_all(copies, AXES, 0, 0, axis_index_groups=groups)]
    ppermute x4 -> x5, starting transfers between devices: 23.9 us -> 25.3 us  [hop(): return lax.ppermute(value, AXES, pairs)]
  transfers between devices with their start and end apart: 9 -> 10, of which waited for: 7 -> 8; matrix products, arithmetic and copies ran while one was open for 1% -> 1% of each run, Pallas kernels for 2% -> 2%
where the time goes in v3:
time: 423 us; the launch traced here: 422 us
  blocking collectives  226 us (53%)
  waiting for transfers between devices  80.5 us (19%)
  starting transfers between devices  57 us (13%)
  Pallas kernels  31.7 us (7%)
  between operations  13.8 us (3%)
  local copies, waits for them, and re-layouts  10.9 us (3%)
    all_to_all x13, blocking collectives, share(): return lax.all_to_all(copies, AXES, 0, 0, axis_index_groups=groups)  226 us
    all_to_all x3, waiting for transfers between devices, share(): return lax.all_to_all(copies, AXES, 0, 0, axis_index_groups=groups)  72.6 us
    all_to_all x3, starting transfers between devices, share(): return lax.all_to_all(copies, AXES, 0, 0, axis_index_groups=groups)  31.6 us
    ppermute x5, starting transfers between devices, hop(): return lax.ppermute(value, AXES, pairs)  25.3 us
    pallas_call x4, Pallas kernels, mix(): pl.pallas_call(kernel, in_specs=[VMEM, VMEM, HBM, VMEM, VMEM], out_specs=...  19.6 us
    pallas_call x4, Pallas kernels, project_out(): pl.pallas_call(kernel, in_specs=[VMEM, HBM, VMEM], out_specs=VMEM, out_sh...  9.97 us
    broadcast_in_dim x16, local copies, waits for them, and re-layouts, share(): copies = jnp.broadcast_to(value[None], (count,) + value.shape)  9.06 us
  transfers between devices with their start and end apart: 10, of which 8 were waited for; matrix products, arithmetic and copies ran while one was open for 1% of the time, Pallas kernels for 2%

profile of v3, /device:TPU:1, one launch (start us, length us, event | category | flops | bytes accessed | tf_op | source)
XLA Modules:
  0.0 422.2 jit_solution(2867701324284702417)
XLA Ops:
  7.4 3.3 collective-permute-start
  11.7 14.2 %conditional.2 = (bf16[4,176,128]{2,1,0:T(8,128)(2,1)S(1)}) conditional(s32[]{:T(128)} %convert_element_type.15, (bf16[176,128]{1,0:T(8,128)(2,1)S(1)}) %tuple.17, bf16[176,128]{1,0:T(8,128)(2,1)S(1)} %broadcast_maximum_fusion), branch_computations={%region_0.1_spmd, %region_1.2_spmd} | conditional | bytes 585736 | solution.py:57
  11.7 14.1 %all_to_all.83 = bf16[4,176,128]{2,1,0:T(8,128)(2,1)S(1)} all-to-all(bf16[4,176,128]{2,1,0:T(8,128)(2,1)S(1)} %broadcast_in_dim.3), channel_id=1, replica_groups={{0,4,8,12},{1,5,9,13},{2,6,10,14},{3,7,11,15},{16,20,24,28},{17,21,25,2..., dimensions={0} | all-to-all | bytes 360448 | tf_op jit(solution)/shard_map/cond/branch_1_fun/all_to_all | solution.py:48
  30.3 6.8 %all-to-all-start.2 = ((bf16[16,4,176,128]{3,2,1,0:T(8,128)(2,1)}), bf16[16,4,176,128]{3,2,1,0:T(8,128)(2,1)S(1)}, u32[]{:S(2)}, u32[]{:S(2)}) async-start(bf16[16,4,176,128]{3,2,1,0:T(8,128)(2,1)} %broadcast_in_dim.56), calls=%async_computation.2 | async-start | bytes 5767168 | tf_op jit(solution)/shard_map/all_to_all | solution.py:48
  40.9 20.0 %all-to-all-done.2.refs_0_ = bf16[16,4,176,128]{3,2,1,0:T(8,128)(2,1)S(1)} async-done(((bf16[16,4,176,128]{3,2,1,0:T(8,128)(2,1)}), bf16[16,4,176,128]{3,2,1,0:T(8,128)(2,1)S(1)}, u32[]{:S(2)}, u32[]{:S(2)}) %all-to-all-start.2) | async-done | bytes 2883616 | tf_op jit(solution)/shard_map/all_to_all | solution.py:48
  62.4 4.8 %mix.4 = bf16[160,128]{1,0:T(8,128)(2,1)S(1)} custom-call(bf16[16,4,176,128]{3,2,1,0:T(8,128)(2,1)S(1)} %all-to-all-done.2.refs_0_, bf16[16,4,16,128]{3,2,1,0:T(8,128)(2,1)S(1)} %slice.76.refs_1_, bf16[2,3,4,4,4,128,128]{6,5,4,3,2,1,0:T(8,128)(2,1)} %bitcast.15, f32[24,128]{1,0:T(8,128)S(1)} %slice.77.refs_3_, bf16[2,8,160,256]{3,2,1,0:T(8,128)(2,1)S(1)} %bitcast.9), custom_call_target="tpu_custom_call" | custom-call | tf_op jit(solution)/shard_map/mix/pallas_call | solution.py:144
  67.3 9.9 %all_to_all.85 = bf16[4,160,128]{2,1,0:T(8,128)(2,1)S(1)} all-to-all(bf16[4,160,128]{2,1,0:T(8,128)(2,1)S(1)} %broadcast_in_dim.58), channel_id=1, replica_groups={{0,4,8,12},{1,5,9,13},{2,6,10,14},{3,7,11,15},{16,20,24,28},{17,21,25,2..., dimensions={0} | all-to-all | bytes 327680 | tf_op jit(solution)/shard_map/all_to_all | solution.py:48
  79.2 14.6 %all-to-all-start.4 = ((bf16[16,4,160,128]{3,2,1,0:T(8,128)(2,1)}), bf16[16,4,160,128]{3,2,1,0:T(8,128)(2,1)S(1)}, u32[]{:S(2)}, u32[]{:S(2)}) async-start(bf16[16,4,160,128]{3,2,1,0:T(8,128)(2,1)} %broadcast_in_dim.59), calls=%async_computation.4 | async-start | bytes 5242880 | tf_op jit(solution)/shard_map/all_to_all | solution.py:48
  93.8 25.6 %all-to-all-done.4.refs_0_ = bf16[16,4,160,128]{3,2,1,0:T(8,128)(2,1)S(1)} async-done(((bf16[16,4,160,128]{3,2,1,0:T(8,128)(2,1)}), bf16[16,4,160,128]{3,2,1,0:T(8,128)(2,1)S(1)}, u32[]{:S(2)}, u32[]{:S(2)}) %all-to-all-start.4) | async-done | bytes 2621472 | tf_op jit(solution)/shard_map/all_to_all | solution.py:48
  119.4 2.5 project_out.4.refs_2_
  121.9 10.5 %all_to_all.86 = bf16[4,160,128]{2,1,0:T(8,128)(2,1)S(1)} all-to-all(bf16[4,160,128]{2,1,0:T(8,128)(2,1)S(1)} %broadcast_in_dim.60), channel_id=1, replica_groups={{0,4,8,12},{1,5,9,13},{2,6,10,14},{3,7,11,15},{16,20,24,28},{17,21,25,2..., dimensions={0} | all-to-all | bytes 327680 | tf_op jit(solution)/shard_map/all_to_all | solution.py:48
  134.5 10.3 %all-to-all-start.6 = ((bf16[16,4,160,128]{3,2,1,0:T(8,128)(2,1)}), bf16[16,4,160,128]{3,2,1,0:T(8,128)(2,1)}, u32[]{:S(2)}, u32[]{:S(2)}) async-start(bf16[16,4,160,128]{3,2,1,0:T(8,128)(2,1)} %broadcast_in_dim.61), calls=%async_computation.6 | async-start | bytes 5242880 | tf_op jit(solution)/shard_map/all_to_all | solution.py:48
  144.8 27.0 %all-to-all-done.6.refs_0_ = bf16[16,4,160,128]{3,2,1,0:T(8,128)(2,1)} async-done(((bf16[16,4,160,128]{3,2,1,0:T(8,128)(2,1)}), bf16[16,4,160,128]{3,2,1,0:T(8,128)(2,1)}, u32[]{:S(2)}, u32[]{:S(2)}) %all-to-all-start.6) | async-done | bytes 2621472 | tf_op jit(solution)/shard_map/all_to_all | solution.py:48
  171.8 6.1 %mix.5 = bf16[160,128]{1,0:T(8,128)(2,1)S(1)} custom-call(bf16[16,4,160,128]{3,2,1,0:T(8,128)(2,1)} %all-to-all-done.6.refs_0_, bf16[16,4,16,128]{3,2,1,0:T(8,128)(2,1)S(1)} %slice.76.refs_1_, bf16[2,3,4,4,4,128,128]{6,5,4,3,2,1,0:T(8,128)(2,1)} %bitcast.16, f32[24,128]{1,0:T(8,128)S(1)} %slice.82.refs_3_, bf16[2,8,160,256]{3,2,1,0:T(8,128)(2,1)S(1)} %bitcast.10), custom_call_target="tpu_custom_call" | custom-call | tf_op jit(solution)/shard_map/mix/pallas_call | solution.py:144
  178.0 9.8 %all_to_all.87 = bf16[4,160,128]{2,1,0:T(8,128)(2,1)S(1)} all-to-all(bf16[4,160,128]{2,1,0:T(8,128)(2,1)S(1)} %broadcast_in_dim.62), channel_id=1, replica_groups={{0,4,8,12},{1,5,9,13},{2,6,10,14},{3,7,11,15},{16,20,24,28},{17,21,25,2..., dimensions={0} | all-to-all | bytes 327680 | tf_op jit(solution)/shard_map/all_to_all | solution.py:48
  188.3 37.7 %all_to_all.88.refs_0_ = bf16[16,4,160,128]{3,2,1,0:T(8,128)(2,1)S(1)} all-to-all(bf16[16,4,160,128]{3,2,1,0:T(8,128)(2,1)S(1)} %broadcast_in_dim.63), channel_id=1, replica_groups={{0,1,2,3,16,17,18,19,32,33,34,35,48,49,50,51},{4,5,6,7,20,21,22,23,36,3..., dimensions={0} | all-to-all | bytes 5242880 | tf_op jit(solution)/shard_map/all_to_all | solution.py:48
  226.0 2.5 project_out.5
  228.5 2.9 collective-permute-start.2
  232.5 11.6 %all_to_all.89 = bf16[4,160,128]{2,1,0:T(8,128)(2,1)S(1)} all-to-all(bf16[4,160,128]{2,1,0:T(8,128)(2,1)S(1)} %broadcast_in_dim.64), channel_id=1, replica_groups={{0,4,8,12},{1,5,9,13},{2,6,10,14},{3,7,11,15},{16,20,24,28},{17,21,25,2..., dimensions={0} | all-to-all | bytes 327680 | tf_op jit(solution)/shard_map/all_to_all | solution.py:48
  244.6 27.8 %all_to_all.90.refs_0_ = bf16[16,4,160,128]{3,2,1,0:T(8,128)(2,1)S(1)} all-to-all(bf16[16,4,160,128]{3,2,1,0:T(8,128)(2,1)S(1)} %broadcast_in_dim.65), channel_id=1, replica_groups={{0,1,2,3,16,17,18,19,32,33,34,35,48,49,50,51},{4,5,6,7,20,21,22,23,36,3..., dimensions={0} | all-to-all | bytes 5242880 | tf_op jit(solution)/shard_map/all_to_all | solution.py:48
  272.4 4.4 %mix.6 = bf16[160,128]{1,0:T(8,128)(2,1)S(1)} custom-call(bf16[16,4,160,128]{3,2,1,0:T(8,128)(2,1)S(1)} %all_to_all.90.refs_0_, bf16[16,4,16,128]{3,2,1,0:T(8,128)(2,1)S(1)} %slice.76.refs_1_, bf16[2,3,4,4,4,128,128]{6,5,4,3,2,1,0:T(8,128)(2,1)} %bitcast.17, f32[24,128]{1,0:T(8,128)S(1)} %slice.77.refs_3_, bf16[2,8,160,256]{3,2,1,0:T(8,128)(2,1)S(1)} %bitcast.11), custom_call_target="tpu_custom_call" | custom-call | tf_op jit(solution)/shard_map/mix/pallas_call | solution.py:144
  276.8 10.5 %all_to_all.91 = bf16[4,160,128]{2,1,0:T(8,128)(2,1)S(1)} all-to-all(bf16[4,160,128]{2,1,0:T(8,128)(2,1)S(1)} %broadcast_in_dim.66), channel_id=1, replica_groups={{0,4,8,12},{1,5,9,13},{2,6,10,14},{3,7,11,15},{16,20,24,28},{17,21,25,2..., dimensions={0} | all-to-all | bytes 327680 | tf_op jit(solution)/shard_map/all_to_all | solution.py:48
  287.8 25.0 %all_to_all.92.refs_0_ = bf16[16,4,160,128]{3,2,1,0:T(8,128)(2,1)S(1)} all-to-all(bf16[16,4,160,128]{3,2,1,0:T(8,128)(2,1)S(1)} %broadcast_in_dim.67), channel_id=1, replica_groups={{0,1,2,3,16,17,18,19,32,33,34,35,48,49,50,51},{4,5,6,7,20,21,22,23,36,3..., dimensions={0} | all-to-all | bytes 5242880 | tf_op jit(solution)/shard_map/all_to_all | solution.py:48
  312.9 2.5 project_out.6.refs_2_
  315.4 11.3 %all_to_all.93 = bf16[4,160,128]{2,1,0:T(8,128)(2,1)S(1)} all-to-all(bf16[4,160,128]{2,1,0:T(8,128)(2,1)S(1)} %broadcast_in_dim.68), channel_id=1, replica_groups={{0,4,8,12},{1,5,9,13},{2,6,10,14},{3,7,11,15},{16,20,24,28},{17,21,25,2..., dimensions={0} | all-to-all | bytes 327680 | tf_op jit(solution)/shard_map/all_to_all | solution.py:48
  327.3 23.9 %all_to_all.94.refs_0_ = bf16[16,4,160,128]{3,2,1,0:T(8,128)(2,1)S(1)} all-to-all(bf16[16,4,160,128]{3,2,1,0:T(8,128)(2,1)S(1)} %broadcast_in_dim.69), channel_id=1, replica_groups={{0,1,2,3,16,17,18,19,32,33,34,35,48,49,50,51},{4,5,6,7,20,21,22,23,36,3..., dimensions={0} | all-to-all | bytes 5242880 | tf_op jit(solution)/shard_map/all_to_all | solution.py:48
  351.2 4.4 %mix.7 = bf16[160,128]{1,0:T(8,128)(2,1)S(1)} custom-call(bf16[16,4,160,128]{3,2,1,0:T(8,128)(2,1)S(1)} %all_to_all.94.refs_0_, bf16[16,4,16,128]{3,2,1,0:T(8,128)(2,1)S(1)} %slice.76.refs_1_, bf16[2,3,4,4,4,128,128]{6,5,4,3,2,1,0:T(8,128)(2,1)} %bitcast.18, f32[24,128]{1,0:T(8,128)S(1)} %slice.82.refs_3_, bf16[2,8,160,256]{3,2,1,0:T(8,128)(2,1)S(1)} %bitcast.12), custom_call_target="tpu_custom_call" | custom-call | tf_op jit(solution)/shard_map/mix/pallas_call | solution.py:144
  355.6 10.7 %all_to_all.95 = bf16[4,160,128]{2,1,0:T(8,128)(2,1)S(1)} all-to-all(bf16[4,160,128]{2,1,0:T(8,128)(2,1)S(1)} %broadcast_in_dim.70), channel_id=1, replica_groups={{0,4,8,12},{1,5,9,13},{2,6,10,14},{3,7,11,15},{16,20,24,28},{17,21,25,2..., dimensions={0} | all-to-all | bytes 327680 | tf_op jit(solution)/shard_map/all_to_all | solution.py:48
  366.8 23.5 %all_to_all.96.refs_0_ = bf16[16,4,160,128]{3,2,1,0:T(8,128)(2,1)S(1)} all-to-all(bf16[16,4,160,128]{3,2,1,0:T(8,128)(2,1)S(1)} %broadcast_in_dim.71), channel_id=1, replica_groups={{0,1,2,3,16,17,18,19,32,33,34,35,48,49,50,51},{4,5,6,7,20,21,22,23,36,3..., dimensions={0} | all-to-all | bytes 5242880 | tf_op jit(solution)/shard_map/all_to_all | solution.py:48
  390.3 2.5 project_out.7
  392.8 16.6 %collective-permute-start.3 = (bf16[2,40,128]{2,1,0:T(8,128)(2,1)S(1)}, bf16[2,40,128]{2,1,0:T(8,128)(2,1)S(1)}, u32[]{:S(2)}, u32[]{:S(2)}) collective-permute-start(bf16[2,40,128]{2,1,0:T(8,128)(2,1)S(1)} %broadcast_select_fusion.2), channel_id=1, source_target_pairs={{0,64},{1,65},{2,66},{3,67},{4,68},{5,69},{6,70},{7,71},{8,72},{9,... | collective-permute-start | bytes 61448 | tf_op jit(solution)/shard_map/ppermute | solution.py:42
  411.5 3.2 collective-permute-done.4
  (79 shorter events, 22.1 us)
Async XLA Ops:
  6.5 4.2 copy-start
  6.5 54.4 %all-gather.3.cloned.1.call-start = ((), (), s32[]{:S(2)}) async-start(), calls=%async_computation.17 | async-start | bytes 18874368 | tf_op jit(solution)/shard_map/all_gather | solution.py:211
  6.5 0.7 copy-start.4
  6.5 0.8 copy-start.5
  6.5 0.8 copy-start.6
  6.6 0.8 copy-start.7
  6.6 4.2 copy-start.8
  7.4 4.2 collective-permute-start
  25.9 2.1 collective-permute-start.1
  30.3 30.6 %all-to-all-start.2 = ((bf16[16,4,176,128]{3,2,1,0:T(8,128)(2,1)}), bf16[16,4,176,128]{3,2,1,0:T(8,128)(2,1)S(1)}, u32[]{:S(2)}, u32[]{:S(2)}) async-start(bf16[16,4,176,128]{3,2,1,0:T(8,128)(2,1)} %broadcast_in_dim.56), calls=%async_computation.2 | async-start | bytes 5767168 | tf_op jit(solution)/shard_map/all_to_all | solution.py:48
  37.1 56.7 %all-gather.5.cloned.1.call-start = ((), (), s32[]{:S(2)}) async-start(), calls=%async_computation.18 | async-start | bytes 6291456 | tf_op jit(solution)/shard_map/all_gather | solution.py:212
  60.9 1.5 copy-start.2
  79.2 40.2 %all-to-all-start.4 = ((bf16[16,4,160,128]{3,2,1,0:T(8,128)(2,1)}), bf16[16,4,160,128]{3,2,1,0:T(8,128)(2,1)S(1)}, u32[]{:S(2)}, u32[]{:S(2)}) async-start(bf16[16,4,160,128]{3,2,1,0:T(8,128)(2,1)} %broadcast_in_dim.59), calls=%async_computation.4 | async-start | bytes 5242880 | tf_op jit(solution)/shard_map/all_to_all | solution.py:48
  134.5 37.3 %copy-start.3 = (bf16[16,160,256]{2,1,0:T(8,128)(2,1)S(1)}, bf16[16,160,256]{2,1,0:T(8,128)(2,1)}, u32[]{:S(2)}) copy-start(bf16[16,160,256]{2,1,0:T(8,128)(2,1)} %toeplitz.1) | copy-start | bytes 3932164
  134.5 37.3 %all-to-all-start.6 = ((bf16[16,4,160,128]{3,2,1,0:T(8,128)(2,1)}), bf16[16,4,160,128]{3,2,1,0:T(8,128)(2,1)}, u32[]{:S(2)}, u32[]{:S(2)}) async-start(bf16[16,4,160,128]{3,2,1,0:T(8,128)(2,1)} %broadcast_in_dim.61), calls=%async_computation.6 | async-start | bytes 5242880 | tf_op jit(solution)/shard_map/all_to_all | solution.py:48
  228.5 4.0 collective-permute-start.2
  366.8 48.6 %copy-start.1 = (bf16[512,128]{1,0:T(8,128)(2,1)S(1)}, bf16[512,128]{1,0:T(8,128)(2,1)}, u32[]{:S(2)}) copy-start(bf16[512,128]{1,0:T(8,128)(2,1)} %param.13) | copy-start | bytes 393220
  392.8 17.4 %collective-permute-start.3 = (bf16[2,40,128]{2,1,0:T(8,128)(2,1)S(1)}, bf16[2,40,128]{2,1,0:T(8,128)(2,1)S(1)}, u32[]{:S(2)}, u32[]{:S(2)}) collective-permute-start(bf16[2,40,128]{2,1,0:T(8,128)(2,1)S(1)} %broadcast_select_fusion.2), channel_id=1, source_target_pairs={{0,64},{1,65},{2,66},{3,67},{4,68},{5,69},{6,70},{7,71},{8,72},{9,... | collective-permute-start | bytes 61448 | tf_op jit(solution)/shard_map/ppermute | solution.py:42
  410.2 4.5 %collective-permute-start.4 = (bf16[2,40,128]{2,1,0:T(8,128)(2,1)S(1)}, bf16[2,40,128]{2,1,0:T(8,128)(2,1)S(1)}, u32[]{:S(2)}, u32[]{:S(2)}) collective-permute-start(bf16[2,40,128]{2,1,0:T(8,128)(2,1)S(1)} %pad_maximum_fusion.2), channel_id=1, source_target_pairs={{128,0},{129,1},{130,2},{131,3},{132,4},{133,5},{134,6},{135,7},{1... | collective-permute-start | bytes 61448 | tf_op jit(solution)/shard_map/ppermute | solution.py:42
Sparse Core Ops, SparseCore 0:
  9.2 34.7 all-gather.2
  45.8 22.0 all-gather.4

commit v4 on v2

--- a/solution.py
+++ b/solution.py
@@ -73,18 +73,33 @@
     )(base)
 
 
-def fetch(layer, weights_ref, held, sems):
-    copies = []
-    for x in range(SIDE):
-        source, target = weights_ref.at[layer, ..., x, :, :, :, :], held.at[..., x, :, :, :, :]
-        copies.append(pltpu.make_async_copy(source, target, sems.at[x]))
-    for copy in copies:
-        copy.start()
-    return copies
-
-
-def mix_kernel(layer, x_ref, gain_ref, w_ref, taps_ref, toep_ref, out_ref, held, sems, total, padded):
-    copies = fetch(layer, w_ref, held, sems)
+def fetch(layer, core_ref, own_ref, other_ref, held, sems):
+    def copies(source):
+        return [
+            pltpu.make_async_copy(
+                source.at[..., x, :, :, :, :], held.at[..., x, :, :, :, :], sems.at[x]
+            )
+            for x in range(SIDE)
+        ]
+
+    @pl.when(core_ref[0] == layer)
+    def _():
+        for copy in copies(own_ref):
+            copy.start()
+
+    @pl.when(core_ref[0] != layer)
+    def _():
+        for copy in copies(other_ref):
+            copy.start()
+
+    return copies(own_ref)
+
+
+def mix_kernel(
+    layer, core_ref, x_ref, gain_ref, own_ref, other_ref, taps_ref, toep_ref, out_ref,
+    held, sems, total, padded,
+):
+    copies = fetch(layer, core_ref, own_ref, other_ref, held, sems)
     power = jnp.zeros((SEQ, LANES), F32)
     for x in range(SIDE):
         scaled = []
@@ -124,17 +139,18 @@
     out_ref[...] = (mixed[0] * carried).astype(BF16)
 
 
+SMEM = pl.BlockSpec(memory_space=pltpu.SMEM)
 VMEM = pl.BlockSpec(memory_space=pltpu.VMEM)
 HBM = pl.BlockSpec(memory_space=pltpu.HBM)
 
 
-def mix(layer, gathered, gains, weights, taps, toep):
+def mix(layer, core, gathered, gains, weights, taps, toep):
     def kernel(*refs):
         mix_kernel(layer, *refs)
 
     return pl.pallas_call(
         kernel,
-        in_specs=[VMEM, VMEM, HBM, VMEM, VMEM],
+        in_specs=[SMEM, VMEM, VMEM, HBM, HBM, VMEM, VMEM],
         out_specs=VMEM,
         out_shape=jax.ShapeDtypeStruct((SEQ, LANES), BF16),
         scratch_shapes=[
@@ -145,11 +161,13 @@
         ],
         compiler_params=pltpu.CompilerParams(vmem_limit_bytes=VMEM_LIMIT),
         name="mix",
-    )(gathered, gains, weights, taps, toep)
-
-
-def out_kernel(layer, g_ref, w_ref, x_ref, out_ref, held, sems, total):
-    copies = fetch(layer, w_ref, held, sems)
+    )(core, gathered, gains, *weights, taps, toep)
+
+
+def out_kernel(
+    layer, core_ref, g_ref, own_ref, other_ref, x_ref, out_ref, held, sems, total
+):
+    copies = fetch(layer, core_ref, own_ref, other_ref, held, sems)
     total[...] = x_ref[...].astype(F32)
     for x in range(SIDE):
         left = jnp.concatenate(
@@ -161,13 +179,13 @@
     out_ref[...] = total[...].astype(BF16)
 
 
-def project_out(layer, gathered, weights, activation):
+def project_out(layer, core, gathered, weights, activation):
     def kernel(*refs):
         out_kernel(layer, *refs)
 
     return pl.pallas_call(
         kernel,
-        in_specs=[VMEM, HBM, VMEM],
+        in_specs=[SMEM, VMEM, HBM, HBM, VMEM],
         out_specs=VMEM,
         out_shape=jax.ShapeDtypeStruct((SEQ, LANES), BF16),
         scratch_shapes=[
@@ -177,14 +195,12 @@
         ],
         compiler_params=pltpu.CompilerParams(vmem_limit_bytes=VMEM_LIMIT),
         name="project_out",
-    )(gathered, weights, activation)
-
-
-CORES = [[0, 1], [2, 3]]
+    )(core, gathered, *weights, activation)
 
 
 def body(tokens, embed, gain, w_in, short_filter, long_filter, skip_bias, w_out):
     core = lax.axis_index("pipe") % 2
+    place_in_chip = jnp.reshape(core, (1,)).astype(jnp.int32)
     swap = [(0, 1), (1, 0), (2, 3), (3, 2)]
 
     own = jnp.concatenate(
@@ -199,10 +215,8 @@
     )
     other = hop(own, swap)
     first, second = jnp.where(core == 0, own, other), jnp.where(core == 0, other, own)
-    w_in_both = lax.all_gather(w_in[0], "pipe", axis_index_groups=CORES)
-    w_out_both = lax.all_gather(w_out[0], "pipe", axis_index_groups=CORES)
-    w_in_both = w_in_both.reshape(2, 3, SIDE, SIDE, SIDE, LANES, LANES)
-    w_out_both = w_out_both.reshape(2, SIDE, SIDE, SIDE, LANES, LANES)
+    w_in_own = w_in.reshape(3, SIDE, SIDE, SIDE, LANES, LANES)
+    w_out_own = w_out.reshape(SIDE, SIDE, SIDE, LANES, LANES)
     rows = 3 * STAPS + 3
     taps = [first[:rows], second[:rows]]
     toep = toeplitz(jnp.concatenate([first[rows:], second[rows:]], axis=0))
@@ -216,16 +230,31 @@
         [first[rows - 2 : rows - 1], second[rows - 2 : rows - 1], jnp.zeros((EXTRA - 2, LANES), F32)],
         axis=0,
     )
-    arrived = gather_channels(jnp.concatenate([activation, gain_rows.astype(BF16)], axis=0))
-    gathered, gains = arrived, arrived[:, :, SEQ:]
-    for part in range(2):
+    def layers(activation, w_in_other, w_out_other):
+        arrived = gather_channels(jnp.concatenate([activation, gain_rows.astype(BF16)], axis=0))
+        gathered, gains = arrived, arrived[:, :, SEQ:]
         for layer in range(2):
-            if part + layer > 0:
+            if layer > 0:
                 gathered = gather_channels(activation)
-            gated = mix(layer, gathered, gains, w_in_both, taps[layer], toep)
-            activation = project_out(layer, gather_channels(gated), w_out_both, activation)
-        if part == 0:
-            activation = hop(activation, [(0, 2), (1, 3)])
+            gated = mix(
+                layer, place_in_chip, gathered, gains, (w_in_own, w_in_other), taps[layer], toep
+            )
+            activation = project_out(
+                layer, place_in_chip, gather_channels(gated), (w_out_own, w_out_other), activation
+            )
+        return activation
+
+    def first_chips(activation):
+        others = hop(w_in_own, swap[:2]), hop(w_out_own, swap[:2])
+        return layers(activation, *others), *others
+
+    def later_chips(activation):
+        return activation, hop(w_in_own, swap[2:]), hop(w_out_own, swap[2:])
+
+    leading = lax.axis_index("pipe") < 2
+    activation, *others = lax.cond(leading, first_chips, later_chips, activation)
+    activation = hop(activation, [(0, 2), (1, 3)])
+    activation = lax.cond(leading, lambda a, *_: a, layers, activation, *others)
 
     quarters = activation.reshape(4, SEQ // 4, LANES)
     even, odd = quarters[0::2], quarters[1::2]

time: 423 us -> 405 us (0.957)
  waiting for transfers between devices: 92.7 us -> 197 us
  blocking collectives: 231 us -> 153 us
  Pallas kernels: 31.3 us -> 17.1 us
  between operations: 13.8 us -> 0.14 us
  starting transfers between devices: 41.1 us -> 27.9 us
  local copies, waits for them, and re-layouts: 10.9 us -> 6.07 us
    ppermute x4 -> x6, waiting for transfers between devices: 5.64 us -> 176 us  [hop(): return lax.ppermute(value, AXES, pairs)]
    all_to_all x13 -> x7, blocking collectives: 231 us -> 153 us  [share(): return lax.all_to_all(copies, AXES, 0, 0, axis_index_groups=groups)]
    all_to_all x3 -> x1, waiting for transfers between devices: 85.6 us -> 20.7 us  [share(): return lax.all_to_all(copies, AXES, 0, 0, axis_index_groups=groups)]
    pallas_call x8 -> x4, Pallas kernels: 29.2 us -> 15 us  [the longest x2 10.7 us: mix(): pl.pallas_call(kernel, in_specs=[SMEM, VMEM, VMEM, HBM, HBM, VMEM, VMEM],...]
    all_to_all x3 -> x1, starting transfers between devices: 17.2 us -> 4.15 us  [share(): return lax.all_to_all(copies, AXES, 0, 0, axis_index_groups=groups)]
    broadcast_in_dim x16 -> x8, local copies, waits for them, and re-layouts: 9.21 us -> 3.68 us  [share(): copies = jnp.broadcast_to(value[None], (count,) + value.shape)]
    ppermute x4 -> x6, starting transfers between devices: 23.9 us -> 23.8 us  [hop(): return lax.ppermute(value, AXES, pairs)]
  transfers between devices with their start and end apart: 9 -> 7, of which waited for: 7 -> 5; matrix products, arithmetic and copies ran while one was open for 1% -> 0% of each run, Pallas kernels for 2% -> 0%
where the time goes in v4:
time: 405 us; the launch traced here: 404 us
  waiting for transfers between devices  197 us (49%)
  blocking collectives  153 us (38%)
  starting transfers between devices  27.9 us (7%)
  Pallas kernels  17.1 us (4%)
  local copies, waits for them, and re-layouts  6.07 us (1%)
    ppermute x6, waiting for transfers between devices, hop(): return lax.ppermute(value, AXES, pairs)  176 us
    all_to_all x7, blocking collectives, share(): return lax.all_to_all(copies, AXES, 0, 0, axis_index_groups=groups)  153 us
    ppermute x6, starting transfers between devices, hop(): return lax.ppermute(value, AXES, pairs)  23.8 us
    all_to_all x1, waiting for transfers between devices, share(): return lax.all_to_all(copies, AXES, 0, 0, axis_index_groups=groups)  20.7 us
    pallas_call x2, Pallas kernels, mix(): pl.pallas_call(kernel, in_specs=[SMEM, VMEM, VMEM, HBM, HBM, VMEM, VMEM],...  10.7 us
  transfers between devices with their start and end apart: 7, of which 5 were waited for; matrix products, arithmetic and copies ran while one was open for 0% of the time, Pallas kernels for 0%

profile of v4, /device:TPU:1, one launch (start us, length us, event | category | flops | bytes accessed | tf_op | source)
XLA Modules:
  0.0 404.0 jit_solution(7312338911530272650)
XLA Ops:
  0.0 0.8 reduce
  0.8 1.4 concatenate.18
  2.2 3.2 collective-permute-start.4
  5.4 0.7 constant_dynamic-slice_fusion
  6.8 0.7 pad_maximum_fusion.3.base_ref
  7.4 2.1 toeplitz.1
  9.7 208.1 %conditional.2 = (bf16[160,128]{1,0:T(8,128)(2,1)S(1)}, bf16[3,4,4,4,128,128]{5,4,3,2,1,0:T(8,128)(2,1)}, bf16[4,4,4,128,128]{4,3,2,1,0:T(8,128)(2,1)}) conditional(s32[]{:T(128)} %convert_element_type.17, (bf16[3,4,4,4,128,128]{5,4,3,2,1,0:T(8,128)(2,1)}, bf16[4,4,4,128,128]{4,3,2,1,0:T(8,128)(2,1)}, bf16[160,128]{1,0:T(8,128)(2,1)S(1)}) %tuple.52, ...), branch_computations={%region_0.1_spmd, %region_1.2_spmd} | conditional | flops 90112 | bytes 124317936 | solution.py:255
  9.7 2.0 collective-permute-start.2
  11.7 13.9 %all_to_all.64 = bf16[4,176,128]{2,1,0:T(8,128)(2,1)S(1)} all-to-all(bf16[4,176,128]{2,1,0:T(8,128)(2,1)S(1)} %broadcast_in_dim.1), channel_id=1, replica_groups={{0,4,8,12},{1,5,9,13},{2,6,10,14},{3,7,11,15},{16,20,24,28},{17,21,25,2..., dimensions={0} | all-to-all | bytes 360448 | tf_op jit(solution)/shard_map/cond/branch_1_fun/all_to_all | solution.py:48
  25.6 0.5 broadcast_in_dim.2
  26.2 40.2 %all_to_all.65.refs_1_ = bf16[16,4,176,128]{3,2,1,0:T(8,128)(2,1)S(1)} all-to-all(bf16[16,4,176,128]{3,2,1,0:T(8,128)(2,1)S(1)} %broadcast_in_dim.2), channel_id=1, replica_groups={{0,1,2,3,16,17,18,19,32,33,34,35,48,49,50,51},{4,5,6,7,20,21,22,23,36,3..., dimensions={0} | all-to-all | bytes 5767168 | tf_op jit(solution)/shard_map/cond/branch_1_fun/all_to_all | solution.py:48
  66.4 5.7 %mix.4 = bf16[160,128]{1,0:T(8,128)(2,1)S(1)} custom-call(s32[1]{0:T(128)} %get-tuple-element.62.refs_0_, bf16[16,4,176,128]{3,2,1,0:T(8,128)(2,1)S(1)} %all_to_all.65.refs_1_, bf16[16,4,16,128]{3,2,1,0:T(8,128)(2,1)S(1)} %slice.80.refs_2_, bf16[3,4,4,4,128,128]{5,4,3,2,1,0:T(8,128)(2,1)S(1)} %copy-done.1, ...), custom_call_target="tpu_custom_call" | custom-call | tf_op jit(solution)/shard_map/cond/branch_1_fun/mix/pallas_call | solution.py:151
  72.2 11.7 %all_to_all.66 = bf16[4,160,128]{2,1,0:T(8,128)(2,1)S(1)} all-to-all(bf16[4,160,128]{2,1,0:T(8,128)(2,1)S(1)} %broadcast_in_dim.3), channel_id=1, replica_groups={{0,4,8,12},{1,5,9,13},{2,6,10,14},{3,7,11,15},{16,20,24,28},{17,21,25,2..., dimensions={0} | all-to-all | bytes 327680 | tf_op jit(solution)/shard_map/cond/branch_1_fun/all_to_all | solution.py:48
  83.8 2.0 broadcast_in_dim.4
  85.9 4.2 %all-to-all-start.3 = ((bf16[16,4,160,128]{3,2,1,0:T(8,128)(2,1)}), bf16[16,4,160,128]{3,2,1,0:T(8,128)(2,1)S(1)}, u32[]{:S(2)}, u32[]{:S(2)}) async-start(bf16[16,4,160,128]{3,2,1,0:T(8,128)(2,1)} %broadcast_in_dim.4), calls=%async_computation.3 | async-start | bytes 5242880 | tf_op jit(solution)/shard_map/cond/branch_1_fun/all_to_all | solution.py:48
  90.0 5.4 %collective-permute-start.3 = (bf16[4,4,4,128,128]{4,3,2,1,0:T(8,128)(2,1)}, bf16[4,4,4,128,128]{4,3,2,1,0:T(8,128)(2,1)}, u32[]{:S(2)}, u32[]{:S(2)}) collective-permute-start(bf16[4,4,4,128,128]{4,3,2,1,0:T(8,128)(2,1)} %get-tuple-element.68.refs_2_), channel_id=1, source_target_pairs={{0,64},{1,65},{2,66},{3,67},{4,68},{5,69},{6,70},{7,71},{8,72},{9,... | collective-permute-start | bytes 6291464 | tf_op jit(solution)/shard_map/cond/branch_1_fun/ppermute | solution.py:42
  95.4 4.1 %collective-permute-done.3.refs_3_ = bf16[4,4,4,128,128]{4,3,2,1,0:T(8,128)(2,1)} collective-permute-done((bf16[4,4,4,128,128]{4,3,2,1,0:T(8,128)(2,1)}, bf16[4,4,4,128,128]{4,3,2,1,0:T(8,128)(2,1)}, u32[]{:S(2)}, u32[]{:S(2)}) %collective-permute-start.3) | collective-permute-done | bytes 2097184 | tf_op jit(solution)/shard_map/cond/branch_1_fun/ppermute | solution.py:42
  99.5 20.7 %all-to-all-done.3.refs_1_ = bf16[16,4,160,128]{3,2,1,0:T(8,128)(2,1)S(1)} async-done(((bf16[16,4,160,128]{3,2,1,0:T(8,128)(2,1)}), bf16[16,4,160,128]{3,2,1,0:T(8,128)(2,1)S(1)}, u32[]{:S(2)}, u32[]{:S(2)}) %all-to-all-start.3) | async-done | bytes 2621472 | tf_op jit(solution)/shard_map/cond/branch_1_fun/all_to_all | solution.py:48
  120.2 2.6 project_out.4.refs_4_
  122.9 9.8 %all_to_all.67 = bf16[4,160,128]{2,1,0:T(8,128)(2,1)S(1)} all-to-all(bf16[4,160,128]{2,1,0:T(8,128)(2,1)S(1)} %broadcast_in_dim.5), channel_id=1, replica_groups={{0,4,8,12},{1,5,9,13},{2,6,10,14},{3,7,11,15},{16,20,24,28},{17,21,25,2..., dimensions={0} | all-to-all | bytes 327680 | tf_op jit(solution)/shard_map/cond/branch_1_fun/all_to_all | solution.py:48
  133.2 37.8 %all_to_all.68.refs_1_ = bf16[16,4,160,128]{3,2,1,0:T(8,128)(2,1)S(1)} all-to-all(bf16[16,4,160,128]{3,2,1,0:T(8,128)(2,1)S(1)} %broadcast_in_dim.6), channel_id=1, replica_groups={{0,1,2,3,16,17,18,19,32,33,34,35,48,49,50,51},{4,5,6,7,20,21,22,23,36,3..., dimensions={0} | all-to-all | bytes 5242880 | tf_op jit(solution)/shard_map/cond/branch_1_fun/all_to_all | solution.py:48
  171.0 5.0 %mix.5 = bf16[160,128]{1,0:T(8,128)(2,1)S(1)} custom-call(s32[1]{0:T(128)} %get-tuple-element.62.refs_0_, bf16[16,4,160,128]{3,2,1,0:T(8,128)(2,1)S(1)} %all_to_all.68.refs_1_, bf16[16,4,16,128]{3,2,1,0:T(8,128)(2,1)S(1)} %slice.80.refs_2_, bf16[3,4,4,4,128,128]{5,4,3,2,1,0:T(8,128)(2,1)S(1)} %bitcast.13, ...), custom_call_target="tpu_custom_call" | custom-call | tf_op jit(solution)/shard_map/cond/branch_1_fun/mix/pallas_call | solution.py:151
  176.0 9.8 %all_to_all.69 = bf16[4,160,128]{2,1,0:T(8,128)(2,1)S(1)} all-to-all(bf16[4,160,128]{2,1,0:T(8,128)(2,1)S(1)} %broadcast_in_dim.7), channel_id=1, replica_groups={{0,4,8,12},{1,5,9,13},{2,6,10,14},{3,7,11,15},{16,20,24,28},{17,21,25,2..., dimensions={0} | all-to-all | bytes 327680 | tf_op jit(solution)/shard_map/cond/branch_1_fun/all_to_all | solution.py:48
  186.3 29.6 %all_to_all.70.refs_1_ = bf16[16,4,160,128]{3,2,1,0:T(8,128)(2,1)S(1)} all-to-all(bf16[16,4,160,128]{3,2,1,0:T(8,128)(2,1)S(1)} %broadcast_in_dim.8), channel_id=1, replica_groups={{0,1,2,3,16,17,18,19,32,33,34,35,48,49,50,51},{4,5,6,7,20,21,22,23,36,3..., dimensions={0} | all-to-all | bytes 5242880 | tf_op jit(solution)/shard_map/cond/branch_1_fun/all_to_all | solution.py:48
  216.0 1.6 project_out.5
  217.8 1.3 collective-permute-start.5
  219.1 1.1 collective-permute-done.5
  220.2 10.6 %collective-permute-start.6 = (bf16[2,40,128]{2,1,0:T(8,128)(2,1)S(1)}, bf16[2,40,128]{2,1,0:T(8,128)(2,1)S(1)}, u32[]{:S(2)}, u32[]{:S(2)}) collective-permute-start(bf16[2,40,128]{2,1,0:T(8,128)(2,1)S(1)} %broadcast_select_fusion.2), channel_id=1, source_target_pairs={{0,64},{1,65},{2,66},{3,67},{4,68},{5,69},{6,70},{7,71},{8,72},{9,... | collective-permute-start | bytes 61448 | tf_op jit(solution)/shard_map/ppermute | solution.py:42
  230.8 0.8 collective-permute-done.6
  231.7 1.3 collective-permute-start.7
  233.0 170.4 %collective-permute-done.7 = bf16[2,40,128]{2,1,0:T(8,128)(2,1)S(1)} collective-permute-done((bf16[2,40,128]{2,1,0:T(8,128)(2,1)S(1)}, bf16[2,40,128]{2,1,0:T(8,128)(2,1)S(1)}, u32[]{:S(2)}, u32[]{:S(2)}) %collective-permute-start.7) | collective-permute-done | bytes 20512 | tf_op jit(solution)/shard_map/ppermute | solution.py:42
  403.4 0.6 maximum_select_fusion
  (46 shorter events, 1.9 us)
Async XLA Ops:
  0.0 6.1 %copy-start = (bf16[512,128]{1,0:T(8,128)(2,1)S(1)}, bf16[512,128]{1,0:T(8,128)(2,1)}, u32[]{:S(2)}) copy-start(bf16[512,128]{1,0:T(8,128)(2,1)} %param.13) | copy-start | bytes 393220
  2.2 4.4 %collective-permute-start.4 = (f32[32,128]{1,0:T(8,128)S(1)}, f32[32,128]{1,0:T(8,128)S(1)}, u32[]{:S(2)}, u32[]{:S(2)}) collective-permute-start(f32[32,128]{1,0:T(8,128)S(1)} %concatenate.18), channel_id=1, source_target_pairs={{0,64},{1,65},{2,66},{3,67},{4,68},{5,69},{6,70},{7,71},{8,72},{9,... | collective-permute-start | bytes 49160 | tf_op jit(solution)/shard_map/ppermute | solution.py:42
  9.7 56.8 %collective-permute-start.2 = (bf16[3,4,4,4,128,128]{5,4,3,2,1,0:T(8,128)(2,1)}, bf16[3,4,4,4,128,128]{5,4,3,2,1,0:T(8,128)(2,1)}, u32[]{:S(2)}, u32[]{:S(2)}) collective-permute-start(bf16[3,4,4,4,128,128]{5,4,3,2,1,0:T(8,128)(2,1)} %get-tuple-element.65.refs_3_), channel_id=1, source_target_pairs={{0,64},{1,65},{2,66},{3,67},{4,68},{5,69},{6,70},{7,71},{8,72},{9,... | collective-permute-start | bytes 18874376 | tf_op jit(solution)/shard_map/cond/branch_1_fun/ppermute | solution.py:42
  26.2 40.2 %copy-start.1 = (bf16[3,4,4,4,128,128]{5,4,3,2,1,0:T(8,128)(2,1)S(1)}, bf16[3,4,4,4,128,128]{5,4,3,2,1,0:T(8,128)(2,1)}, u32[]{:S(2)}) copy-start(bf16[3,4,4,4,128,128]{5,4,3,2,1,0:T(8,128)(2,1)} %get-tuple-element.65.refs_3_) | copy-start | bytes 18874372 | tf_op jit(solution)/shard_map/cond
  85.9 34.4 %all-to-all-start.3 = ((bf16[16,4,160,128]{3,2,1,0:T(8,128)(2,1)}), bf16[16,4,160,128]{3,2,1,0:T(8,128)(2,1)S(1)}, u32[]{:S(2)}, u32[]{:S(2)}) async-start(bf16[16,4,160,128]{3,2,1,0:T(8,128)(2,1)} %broadcast_in_dim.4), calls=%async_computation.3 | async-start | bytes 5242880 | tf_op jit(solution)/shard_map/cond/branch_1_fun/all_to_all | solution.py:48
  90.0 9.5 %collective-permute-start.3 = (bf16[4,4,4,128,128]{4,3,2,1,0:T(8,128)(2,1)}, bf16[4,4,4,128,128]{4,3,2,1,0:T(8,128)(2,1)}, u32[]{:S(2)}, u32[]{:S(2)}) collective-permute-start(bf16[4,4,4,128,128]{4,3,2,1,0:T(8,128)(2,1)} %get-tuple-element.68.refs_2_), channel_id=1, source_target_pairs={{0,64},{1,65},{2,66},{3,67},{4,68},{5,69},{6,70},{7,71},{8,72},{9,... | collective-permute-start | bytes 6291464 | tf_op jit(solution)/shard_map/cond/branch_1_fun/ppermute | solution.py:42
  120.2 50.7 %slice-start = ((s8[6291456]{0:T(1024)(128)(4,1)}), s8[4194304]{0:T(1024)(128)(4,1)S(1)}, s32[]{:S(2)}) async-start(s8[6291456]{0:T(1024)(128)(4,1)} %bitcast.12), calls=%async_computation.16 | async-start | bytes 8388608 | tf_op jit(solution)/shard_map/cond
  132.7 38.3 %slice-start.1 = ((s8[6291456]{0:T(1024)(128)(4,1)}), s8[2097152]{0:T(1024)(128)(4,1)S(1)}, s32[]{:S(2)}) async-start(s8[6291456]{0:T(1024)(128)(4,1)} %bitcast.12), calls=%async_computation.17 | async-start | bytes 4194304 | tf_op jit(solution)/shard_map/cond
  186.3 29.7 %copy-start.3 = (bf16[4,4,4,128,128]{4,3,2,1,0:T(8,128)(2,1)S(1)}, bf16[4,4,4,128,128]{4,3,2,1,0:T(8,128)(2,1)}, u32[]{:S(2)}) copy-start(bf16[4,4,4,128,128]{4,3,2,1,0:T(8,128)(2,1)} %get-tuple-element.68.refs_2_) | copy-start | bytes 6291460 | tf_op jit(solution)/shard_map/cond
  217.8 2.4 collective-permute-start.5
  220.2 11.5 %collective-permute-start.6 = (bf16[2,40,128]{2,1,0:T(8,128)(2,1)S(1)}, bf16[2,40,128]{2,1,0:T(8,128)(2,1)S(1)}, u32[]{:S(2)}, u32[]{:S(2)}) collective-permute-start(bf16[2,40,128]{2,1,0:T(8,128)(2,1)S(1)} %broadcast_select_fusion.2), channel_id=1, source_target_pairs={{0,64},{1,65},{2,66},{3,67},{4,68},{5,69},{6,70},{7,71},{8,72},{9,... | collective-permute-start | bytes 61448 | tf_op jit(solution)/shard_map/ppermute | solution.py:42
  231.7 171.7 %collective-permute-start.7 = (bf16[2,40,128]{2,1,0:T(8,128)(2,1)S(1)}, bf16[2,40,128]{2,1,0:T(8,128)(2,1)S(1)}, u32[]{:S(2)}, u32[]{:S(2)}) collective-permute-start(bf16[2,40,128]{2,1,0:T(8,128)(2,1)S(1)} %pad_maximum_fusion.2), channel_id=1, source_target_pairs={{128,0},{129,1},{130,2},{131,3},{132,4},{133,5},{134,6},{135,7},{1... | collective-permute-start | bytes 61448 | tf_op jit(solution)/shard_map/ppermute | solution.py:42

commit v5 on v4

--- a/solution.py
+++ b/solution.py
@@ -230,8 +230,10 @@
         [first[rows - 2 : rows - 1], second[rows - 2 : rows - 1], jnp.zeros((EXTRA - 2, LANES), F32)],
         axis=0,
     )
-    def layers(activation, w_in_other, w_out_other):
-        arrived = gather_channels(jnp.concatenate([activation, gain_rows.astype(BF16)], axis=0))
+    def with_gains(activation):
+        return jnp.concatenate([activation, gain_rows.astype(BF16)], axis=0)
+
+    def layers(arrived, activation, w_in_other, w_out_other):
         gathered, gains = arrived, arrived[:, :, SEQ:]
         for layer in range(2):
             if layer > 0:
@@ -245,8 +247,13 @@
         return activation
 
     def first_chips(activation):
+        block = with_gains(activation)
         others = hop(w_in_own, swap[:2]), hop(w_out_own, swap[:2])
-        return layers(activation, *others), *others
+        shape = (SIDE * SIDE, SIDE) + block.shape
+        ahead = lax.cond(core == 1, gather_channels, lambda b: jnp.zeros(shape, BF16), block)
+        block, ahead, *others = lax.optimization_barrier((block, ahead, *others))
+        arrived = lax.cond(core == 0, lambda b, a: gather_channels(b), lambda b, a: a, block, ahead)
+        return layers(arrived, activation, *others), *others
 
     def later_chips(activation):
         return activation, hop(w_in_own, swap[2:]), hop(w_out_own, swap[2:])
@@ -254,7 +261,13 @@
     leading = lax.axis_index("pipe") < 2
     activation, *others = lax.cond(leading, first_chips, later_chips, activation)
     activation = hop(activation, [(0, 2), (1, 3)])
-    activation = lax.cond(leading, lambda a, *_: a, layers, activation, *others)
+    activation = lax.cond(
+        leading,
+        lambda a, *_: a,
+        lambda a, *o: layers(gather_channels(with_gains(a)), a, *o),
+        activation,
+        *others,
+    )
 
     quarters = activation.reshape(4, SEQ // 4, LANES)
     even, odd = quarters[0::2], quarters[1::2]

time: 405 us -> 384 us (0.948)
  waiting for transfers between devices: 197 us -> 182 us
  blocking collectives: 153 us -> 144 us
  starting transfers between devices: 27.9 us -> 34.1 us
    all_to_all x1 -> x0, waiting for transfers between devices: 20.7 us -> none  [share(): return lax.all_to_all(copies, AXES, 0, 0, axis_index_groups=groups)]
    ppermute x6, starting transfers between devices: 23.8 us -> 34.1 us  [hop(): return lax.ppermute(value, AXES, pairs)]
    all_to_all x7 -> x8, blocking collectives: 153 us -> 144 us  [share(): return lax.all_to_all(copies, AXES, 0, 0, axis_index_groups=groups)]
    ppermute x6, waiting for transfers between devices: 176 us -> 182 us  [hop(): return lax.ppermute(value, AXES, pairs)]
    all_to_all x1 -> x0, starting transfers between devices: 4.15 us -> none  [share(): return lax.all_to_all(copies, AXES, 0, 0, axis_index_groups=groups)]
  transfers between devices with their start and end apart: 7 -> 6, of which waited for: 5 -> 3; matrix products, arithmetic and copies ran while one was open for 0% -> 0% of each run, Pallas kernels for 0% -> 0%
where the time goes in v5:
time: 384 us; the launch traced here: 383 us
  waiting for transfers between devices  182 us (47%)
  blocking collectives  144 us (38%)
  starting transfers between devices  34.1 us (9%)
  Pallas kernels  15.4 us (4%)
  local copies, waits for them, and re-layouts  5.49 us (1%)
    ppermute x6, waiting for transfers between devices, hop(): return lax.ppermute(value, AXES, pairs)  182 us
    all_to_all x8, blocking collectives, share(): return lax.all_to_all(copies, AXES, 0, 0, axis_index_groups=groups)  144 us
    ppermute x6, starting transfers between devices, hop(): return lax.ppermute(value, AXES, pairs)  34.1 us
    pallas_call x2, Pallas kernels, mix(): pl.pallas_call(kernel, in_specs=[SMEM, VMEM, VMEM, HBM, HBM, VMEM, VMEM],...  10.1 us
  transfers between devices with their start and end apart: 6, of which 3 were waited for; matrix products, arithmetic and copies ran while one was open for 0% of the time, Pallas kernels for 0%

profile of v5, /device:TPU:1, one launch (start us, length us, event | category | flops | bytes accessed | tf_op | source)
XLA Modules:
  0.0 383.3 jit_solution(17593564741591430078)
XLA Ops:
  0.0 0.8 reduce
  0.8 1.4 concatenate.21
  2.2 3.2 collective-permute-start.4
  5.4 0.7 constant_dynamic-slice_fusion
  6.8 0.7 pad_maximum_fusion.3.base_ref
  7.4 1.1 toeplitz.1
  8.6 165.8 %conditional.4 = (bf16[160,128]{1,0:T(8,128)(2,1)S(1)}, bf16[3,4,4,4,128,128]{5,4,3,2,1,0:T(8,128)(2,1)}, bf16[4,4,4,128,128]{4,3,2,1,0:T(8,128)(2,1)}) conditional(s32[]{:T(128)} %convert_element_type.23, (bf16[3,4,4,4,128,128]{5,4,3,2,1,0:T(8,128)(2,1)}, bf16[4,4,4,128,128]{4,3,2,1,0:T(8,128)(2,1)}, bf16[160,128]{1,0:T(8,128)(2,1)S(1)}) %tuple.79, ...), branch_computations={%region_0.1_spmd, %region_1.6_spmd} | conditional | flops 90116 | bytes 105947360 | solution.py:262
  8.6 2.0 collective-permute-start.2
  10.6 2.4 collective-permute-start.3
  12.9 44.5 %conditional = (bf16[16,4,176,128]{3,2,1,0:T(8,128)(2,1)}) conditional(s32[]{:T(128)} %convert_element_type.18, () %tuple.46, bf16[176,128]{1,0:T(8,128)(2,1)S(1)} %pad_maximum_fusion), branch_computations={%region_2.2_spmd, %region_3.3_spmd} | conditional | bytes 9416712 | solution.py:253
  13.0 14.1 %all_to_all.72 = bf16[4,176,128]{2,1,0:T(8,128)(2,1)S(1)} all-to-all(bf16[4,176,128]{2,1,0:T(8,128)(2,1)S(1)} %broadcast_in_dim.24), channel_id=1, replica_groups={{0,4,8,12},{1,5,9,13},{2,6,10,14},{3,7,11,15},{16,20,24,28},{17,21,25,2..., dimensions={0} | all-to-all | bytes 360448 | tf_op jit(solution)/shard_map/cond/branch_1_fun/cond/branch_1_fun/all_to_all | solution.py:48
  27.1 0.5 broadcast_in_dim.25
  27.6 29.8 %all_to_all.73 = bf16[16,4,176,128]{3,2,1,0:T(8,128)(2,1)} all-to-all(bf16[16,4,176,128]{3,2,1,0:T(8,128)(2,1)S(1)} %broadcast_in_dim.25), channel_id=1, replica_groups={{0,1,2,3,16,17,18,19,32,33,34,35,48,49,50,51},{4,5,6,7,20,21,22,23,36,3..., dimensions={0} | all-to-all | bytes 5767168 | tf_op jit(solution)/shard_map/cond/branch_1_fun/cond/branch_1_fun/all_to_all | solution.py:48
  57.5 1.0 slice.80.refs_2_
  58.5 6.2 %mix.4 = bf16[160,128]{1,0:T(8,128)(2,1)S(1)} custom-call(s32[1]{0:T(128)} %get-tuple-element.79.refs_0_, bf16[16,4,176,128]{3,2,1,0:T(8,128)(2,1)} %get-tuple-element.135.refs_1_, bf16[16,4,16,128]{3,2,1,0:T(8,128)(2,1)S(1)} %slice.80.refs_2_, bf16[3,4,4,4,128,128]{5,4,3,2,1,0:T(8,128)(2,1)} %get-tuple-element.83.refs_3_, ...), custom_call_target="tpu_custom_call" | custom-call | tf_op jit(solution)/shard_map/cond/branch_1_fun/mix/pallas_call | solution.py:151
  64.7 9.8 %all_to_all.76 = bf16[4,160,128]{2,1,0:T(8,128)(2,1)S(1)} all-to-all(bf16[4,160,128]{2,1,0:T(8,128)(2,1)S(1)} %broadcast_in_dim.28), channel_id=1, replica_groups={{0,4,8,12},{1,5,9,13},{2,6,10,14},{3,7,11,15},{16,20,24,28},{17,21,25,2..., dimensions={0} | all-to-all | bytes 327680 | tf_op jit(solution)/shard_map/cond/branch_1_fun/all_to_all | solution.py:48
  74.5 0.5 broadcast_in_dim.42
  75.0 23.9 %all_to_all.77.refs_1_ = bf16[16,4,160,128]{3,2,1,0:T(8,128)(2,1)S(1)} all-to-all(bf16[16,4,160,128]{3,2,1,0:T(8,128)(2,1)S(1)} %broadcast_in_dim.42), channel_id=1, replica_groups={{0,1,2,3,16,17,18,19,32,33,34,35,48,49,50,51},{4,5,6,7,20,21,22,23,36,3..., dimensions={0} | all-to-all | bytes 5242880 | tf_op jit(solution)/shard_map/cond/branch_1_fun/all_to_all | solution.py:48
  98.9 2.6 project_out.4.refs_4_
  101.6 10.1 %all_to_all.78 = bf16[4,160,128]{2,1,0:T(8,128)(2,1)S(1)} all-to-all(bf16[4,160,128]{2,1,0:T(8,128)(2,1)S(1)} %broadcast_in_dim.43), channel_id=1, replica_groups={{0,4,8,12},{1,5,9,13},{2,6,10,14},{3,7,11,15},{16,20,24,28},{17,21,25,2..., dimensions={0} | all-to-all | bytes 327680 | tf_op jit(solution)/shard_map/cond/branch_1_fun/all_to_all | solution.py:48
  112.2 23.0 %all_to_all.79.refs_1_ = bf16[16,4,160,128]{3,2,1,0:T(8,128)(2,1)S(1)} all-to-all(bf16[16,4,160,128]{3,2,1,0:T(8,128)(2,1)S(1)} %broadcast_in_dim.44), channel_id=1, replica_groups={{0,1,2,3,16,17,18,19,32,33,34,35,48,49,50,51},{4,5,6,7,20,21,22,23,36,3..., dimensions={0} | all-to-all | bytes 5242880 | tf_op jit(solution)/shard_map/cond/branch_1_fun/all_to_all | solution.py:48
  135.2 3.9 %mix.5 = bf16[160,128]{1,0:T(8,128)(2,1)S(1)} custom-call(s32[1]{0:T(128)} %get-tuple-element.79.refs_0_, bf16[16,4,160,128]{3,2,1,0:T(8,128)(2,1)S(1)} %all_to_all.79.refs_1_, bf16[16,4,16,128]{3,2,1,0:T(8,128)(2,1)S(1)} %slice.80.refs_2_, bf16[3,4,4,4,128,128]{5,4,3,2,1,0:T(8,128)(2,1)S(1)} %bitcast.13, ...), custom_call_target="tpu_custom_call" | custom-call | tf_op jit(solution)/shard_map/cond/branch_1_fun/mix/pallas_call | solution.py:151
  139.1 9.9 %all_to_all.80 = bf16[4,160,128]{2,1,0:T(8,128)(2,1)S(1)} all-to-all(bf16[4,160,128]{2,1,0:T(8,128)(2,1)S(1)} %broadcast_in_dim.45), channel_id=1, replica_groups={{0,4,8,12},{1,5,9,13},{2,6,10,14},{3,7,11,15},{16,20,24,28},{17,21,25,2..., dimensions={0} | all-to-all | bytes 327680 | tf_op jit(solution)/shard_map/cond/branch_1_fun/all_to_all | solution.py:48
  149.6 23.0 %all_to_all.81.refs_1_ = bf16[16,4,160,128]{3,2,1,0:T(8,128)(2,1)S(1)} all-to-all(bf16[16,4,160,128]{3,2,1,0:T(8,128)(2,1)S(1)} %broadcast_in_dim.46), channel_id=1, replica_groups={{0,1,2,3,16,17,18,19,32,33,34,35,48,49,50,51},{4,5,6,7,20,21,22,23,36,3..., dimensions={0} | all-to-all | bytes 5242880 | tf_op jit(solution)/shard_map/cond/branch_1_fun/all_to_all | solution.py:48
  172.5 1.6 project_out.5
  174.4 1.3 collective-permute-start.5
  175.7 1.1 collective-permute-done.5
  176.8 23.9 %collective-permute-start.6 = (bf16[2,40,128]{2,1,0:T(8,128)(2,1)S(1)}, bf16[2,40,128]{2,1,0:T(8,128)(2,1)S(1)}, u32[]{:S(2)}, u32[]{:S(2)}) collective-permute-start(bf16[2,40,128]{2,1,0:T(8,128)(2,1)S(1)} %broadcast_select_fusion.2), channel_id=1, source_target_pairs={{0,64},{1,65},{2,66},{3,67},{4,68},{5,69},{6,70},{7,71},{8,72},{9,... | collective-permute-start | bytes 61448 | tf_op jit(solution)/shard_map/ppermute | solution.py:42
  200.7 0.8 collective-permute-done.6
  201.6 1.3 collective-permute-start.7
  202.9 179.8 %collective-permute-done.7 = bf16[2,40,128]{2,1,0:T(8,128)(2,1)S(1)} collective-permute-done((bf16[2,40,128]{2,1,0:T(8,128)(2,1)S(1)}, bf16[2,40,128]{2,1,0:T(8,128)(2,1)S(1)}, u32[]{:S(2)}, u32[]{:S(2)}) %collective-permute-start.7) | collective-permute-done | bytes 20512 | tf_op jit(solution)/shard_map/ppermute | solution.py:42
  382.7 0.6 maximum_select_fusion
  (47 shorter events, 1.8 us)
Async XLA Ops:
  0.0 6.1 %copy-start = (bf16[512,128]{1,0:T(8,128)(2,1)S(1)}, bf16[512,128]{1,0:T(8,128)(2,1)}, u32[]{:S(2)}) copy-start(bf16[512,128]{1,0:T(8,128)(2,1)} %param.17) | copy-start | bytes 393220
  2.2 4.4 %collective-permute-start.4 = (f32[32,128]{1,0:T(8,128)S(1)}, f32[32,128]{1,0:T(8,128)S(1)}, u32[]{:S(2)}, u32[]{:S(2)}) collective-permute-start(f32[32,128]{1,0:T(8,128)S(1)} %concatenate.21), channel_id=1, source_target_pairs={{0,64},{1,65},{2,66},{3,67},{4,68},{5,69},{6,70},{7,71},{8,72},{9,... | collective-permute-start | bytes 49160 | tf_op jit(solution)/shard_map/ppermute | solution.py:42
  8.6 48.9 %collective-permute-start.2 = (bf16[3,4,4,4,128,128]{5,4,3,2,1,0:T(8,128)(2,1)}, bf16[3,4,4,4,128,128]{5,4,3,2,1,0:T(8,128)(2,1)}, u32[]{:S(2)}, u32[]{:S(2)}) collective-permute-start(bf16[3,4,4,4,128,128]{5,4,3,2,1,0:T(8,128)(2,1)} %get-tuple-element.83.refs_3_), channel_id=1, source_target_pairs={{0,64},{1,65},{2,66},{3,67},{4,68},{5,69},{6,70},{7,71},{8,72},{9,... | collective-permute-start | bytes 18874376 | tf_op jit(solution)/shard_map/cond/branch_1_fun/ppermute | solution.py:42
  10.6 46.9 %collective-permute-start.3 = (bf16[4,4,4,128,128]{4,3,2,1,0:T(8,128)(2,1)}, bf16[4,4,4,128,128]{4,3,2,1,0:T(8,128)(2,1)}, u32[]{:S(2)}, u32[]{:S(2)}) collective-permute-start(bf16[4,4,4,128,128]{4,3,2,1,0:T(8,128)(2,1)} %get-tuple-element.84.refs_2_), channel_id=1, source_target_pairs={{0,64},{1,65},{2,66},{3,67},{4,68},{5,69},{6,70},{7,71},{8,72},{9,... | collective-permute-start | bytes 6291464 | tf_op jit(solution)/shard_map/cond/branch_1_fun/ppermute | solution.py:42
  75.0 23.9 %copy-start.3 = (bf16[4,4,4,128,128]{4,3,2,1,0:T(8,128)(2,1)S(1)}, bf16[4,4,4,128,128]{4,3,2,1,0:T(8,128)(2,1)}, u32[]{:S(2)}) copy-start(bf16[4,4,4,128,128]{4,3,2,1,0:T(8,128)(2,1)} %get-tuple-element.84.refs_2_) | copy-start | bytes 6291460 | tf_op jit(solution)/shard_map/cond
  98.9 36.3 %slice-start = ((s8[6291456]{0:T(1024)(128)(4,1)}), s8[4194304]{0:T(1024)(128)(4,1)S(1)}, s32[]{:S(2)}) async-start(s8[6291456]{0:T(1024)(128)(4,1)} %bitcast.12), calls=%async_computation.18 | async-start | bytes 8388608 | tf_op jit(solution)/shard_map/cond
  111.7 23.5 %slice-start.1 = ((s8[6291456]{0:T(1024)(128)(4,1)}), s8[2097152]{0:T(1024)(128)(4,1)S(1)}, s32[]{:S(2)}) async-start(s8[6291456]{0:T(1024)(128)(4,1)} %bitcast.12), calls=%async_computation.19 | async-start | bytes 4194304 | tf_op jit(solution)/shard_map/cond
  174.4 2.4 collective-permute-start.5
  176.8 206.5 %copy-start.1 = (bf16[512,128]{1,0:T(8,128)(2,1)S(1)}, bf16[512,128]{1,0:T(8,128)(2,1)}, u32[]{:S(2)}) copy-start(bf16[512,128]{1,0:T(8,128)(2,1)} %param.17) | copy-start | bytes 393220
  176.8 24.7 %collective-permute-start.6 = (bf16[2,40,128]{2,1,0:T(8,128)(2,1)S(1)}, bf16[2,40,128]{2,1,0:T(8,128)(2,1)S(1)}, u32[]{:S(2)}, u32[]{:S(2)}) collective-permute-start(bf16[2,40,128]{2,1,0:T(8,128)(2,1)S(1)} %broadcast_select_fusion.2), channel_id=1, source_target_pairs={{0,64},{1,65},{2,66},{3,67},{4,68},{5,69},{6,70},{7,71},{8,72},{9,... | collective-permute-start | bytes 61448 | tf_op jit(solution)/shard_map/ppermute | solution.py:42
  201.6 181.1 %collective-permute-start.7 = (bf16[2,40,128]{2,1,0:T(8,128)(2,1)S(1)}, bf16[2,40,128]{2,1,0:T(8,128)(2,1)S(1)}, u32[]{:S(2)}, u32[]{:S(2)}) collective-permute-start(bf16[2,40,128]{2,1,0:T(8,128)(2,1)S(1)} %pad_maximum_fusion.2), channel_id=1, source_target_pairs={{128,0},{129,1},{130,2},{131,3},{132,4},{133,5},{134,6},{135,7},{1... | collective-permute-start | bytes 61448 | tf_op jit(solution)/shard_map/ppermute | solution.py:42

commit v6 on v5

--- a/solution.py
+++ b/solution.py
@@ -260,7 +260,7 @@
 
     leading = lax.axis_index("pipe") < 2
     activation, *others = lax.cond(leading, first_chips, later_chips, activation)
-    activation = hop(activation, [(0, 2), (1, 3)])
+    activation = hop(activation, [(0, 3), (1, 2)])
     activation = lax.cond(
         leading,
         lambda a, *_: a,
@@ -273,7 +273,7 @@
     even, odd = quarters[0::2], quarters[1::2]
     keep = jnp.where(core == 0, even, odd)
     taken = hop(jnp.where(core == 0, odd, even), swap)
-    row_0, row_1 = jnp.where(core == 0, keep, taken), jnp.where(core == 0, taken, keep)
+    row_0, row_1 = jnp.where(core == 0, taken, keep), jnp.where(core == 0, keep, taken)
     low, high = jnp.stack([row_0[0], row_1[0]]), jnp.stack([row_0[1], row_1[1]])
     passed = hop(low, [(2, 0), (3, 1)])
     return jnp.where(lax.axis_index("pipe") < 2, passed, high)

time: 384 us -> 357 us (0.930)
  waiting for transfers between devices: 182 us -> 155 us
    ppermute x6, waiting for transfers between devices: 182 us -> 155 us  [hop(): return lax.ppermute(value, AXES, pairs)]
where the time goes in v6:
time: 357 us; the launch traced here: 356 us
  waiting for transfers between devices  155 us (43%)
  blocking collectives  144 us (40%)
  starting transfers between devices  34.1 us (10%)
  Pallas kernels  15.4 us (4%)
  local copies, waits for them, and re-layouts  5.49 us (2%)
    ppermute x6, waiting for transfers between devices, hop(): return lax.ppermute(value, AXES, pairs)  155 us
    all_to_all x8, blocking collectives, share(): return lax.all_to_all(copies, AXES, 0, 0, axis_index_groups=groups)  144 us
    ppermute x6, starting transfers between devices, hop(): return lax.ppermute(value, AXES, pairs)  34.1 us
    pallas_call x2, Pallas kernels, mix(): pl.pallas_call(kernel, in_specs=[SMEM, VMEM, VMEM, HBM, HBM, VMEM, VMEM],...  10.1 us
  transfers between devices with their start and end apart: 6, of which 3 were waited for; matrix products, arithmetic and copies ran while one was open for 0% of the time, Pallas kernels for 0%

profile of v6, /device:TPU:1, one launch (start us, length us, event | category | flops | bytes accessed | tf_op | source)
XLA Modules:
  0.0 356.3 jit_solution(17430498853086191896)
XLA Ops:
  0.0 0.8 reduce
  0.8 1.4 concatenate.21
  2.2 3.2 collective-permute-start.4
  5.4 0.7 constant_dynamic-slice_fusion
  6.8 0.7 pad_maximum_fusion.3.base_ref
  7.4 1.1 toeplitz.1
  8.6 165.8 %conditional.4 = (bf16[160,128]{1,0:T(8,128)(2,1)S(1)}, bf16[3,4,4,4,128,128]{5,4,3,2,1,0:T(8,128)(2,1)}, bf16[4,4,4,128,128]{4,3,2,1,0:T(8,128)(2,1)}) conditional(s32[]{:T(128)} %convert_element_type.23, (bf16[3,4,4,4,128,128]{5,4,3,2,1,0:T(8,128)(2,1)}, bf16[4,4,4,128,128]{4,3,2,1,0:T(8,128)(2,1)}, bf16[160,128]{1,0:T(8,128)(2,1)S(1)}) %tuple.79, ...), branch_computations={%region_0.1_spmd, %region_1.6_spmd} | conditional | flops 90116 | bytes 105947360 | solution.py:262
  8.6 2.0 collective-permute-start.2
  10.6 2.4 collective-permute-start.3
  12.9 44.5 %conditional = (bf16[16,4,176,128]{3,2,1,0:T(8,128)(2,1)}) conditional(s32[]{:T(128)} %convert_element_type.18, () %tuple.46, bf16[176,128]{1,0:T(8,128)(2,1)S(1)} %pad_maximum_fusion), branch_computations={%region_2.2_spmd, %region_3.3_spmd} | conditional | bytes 9416712 | solution.py:253
  13.0 14.1 %all_to_all.72 = bf16[4,176,128]{2,1,0:T(8,128)(2,1)S(1)} all-to-all(bf16[4,176,128]{2,1,0:T(8,128)(2,1)S(1)} %broadcast_in_dim.24), channel_id=1, replica_groups={{0,4,8,12},{1,5,9,13},{2,6,10,14},{3,7,11,15},{16,20,24,28},{17,21,25,2..., dimensions={0} | all-to-all | bytes 360448 | tf_op jit(solution)/shard_map/cond/branch_1_fun/cond/branch_1_fun/all_to_all | solution.py:48
  27.1 0.5 broadcast_in_dim.25
  27.6 29.8 %all_to_all.73 = bf16[16,4,176,128]{3,2,1,0:T(8,128)(2,1)} all-to-all(bf16[16,4,176,128]{3,2,1,0:T(8,128)(2,1)S(1)} %broadcast_in_dim.25), channel_id=1, replica_groups={{0,1,2,3,16,17,18,19,32,33,34,35,48,49,50,51},{4,5,6,7,20,21,22,23,36,3..., dimensions={0} | all-to-all | bytes 5767168 | tf_op jit(solution)/shard_map/cond/branch_1_fun/cond/branch_1_fun/all_to_all | solution.py:48
  57.5 1.0 slice.80.refs_2_
  58.5 6.2 %mix.4 = bf16[160,128]{1,0:T(8,128)(2,1)S(1)} custom-call(s32[1]{0:T(128)} %get-tuple-element.79.refs_0_, bf16[16,4,176,128]{3,2,1,0:T(8,128)(2,1)} %get-tuple-element.135.refs_1_, bf16[16,4,16,128]{3,2,1,0:T(8,128)(2,1)S(1)} %slice.80.refs_2_, bf16[3,4,4,4,128,128]{5,4,3,2,1,0:T(8,128)(2,1)} %get-tuple-element.83.refs_3_, ...), custom_call_target="tpu_custom_call" | custom-call | tf_op jit(solution)/shard_map/cond/branch_1_fun/mix/pallas_call | solution.py:151
  64.7 9.8 %all_to_all.76 = bf16[4,160,128]{2,1,0:T(8,128)(2,1)S(1)} all-to-all(bf16[4,160,128]{2,1,0:T(8,128)(2,1)S(1)} %broadcast_in_dim.28), channel_id=1, replica_groups={{0,4,8,12},{1,5,9,13},{2,6,10,14},{3,7,11,15},{16,20,24,28},{17,21,25,2..., dimensions={0} | all-to-all | bytes 327680 | tf_op jit(solution)/shard_map/cond/branch_1_fun/all_to_all | solution.py:48
  74.5 0.5 broadcast_in_dim.42
  75.0 23.9 %all_to_all.77.refs_1_ = bf16[16,4,160,128]{3,2,1,0:T(8,128)(2,1)S(1)} all-to-all(bf16[16,4,160,128]{3,2,1,0:T(8,128)(2,1)S(1)} %broadcast_in_dim.42), channel_id=1, replica_groups={{0,1,2,3,16,17,18,19,32,33,34,35,48,49,50,51},{4,5,6,7,20,21,22,23,36,3..., dimensions={0} | all-to-all | bytes 5242880 | tf_op jit(solution)/shard_map/cond/branch_1_fun/all_to_all | solution.py:48
  98.9 2.6 project_out.4.refs_4_
  101.6 10.1 %all_to_all.78 = bf16[4,160,128]{2,1,0:T(8,128)(2,1)S(1)} all-to-all(bf16[4,160,128]{2,1,0:T(8,128)(2,1)S(1)} %broadcast_in_dim.43), channel_id=1, replica_groups={{0,4,8,12},{1,5,9,13},{2,6,10,14},{3,7,11,15},{16,20,24,28},{17,21,25,2..., dimensions={0} | all-to-all | bytes 327680 | tf_op jit(solution)/shard_map/cond/branch_1_fun/all_to_all | solution.py:48
  112.2 23.0 %all_to_all.79.refs_1_ = bf16[16,4,160,128]{3,2,1,0:T(8,128)(2,1)S(1)} all-to-all(bf16[16,4,160,128]{3,2,1,0:T(8,128)(2,1)S(1)} %broadcast_in_dim.44), channel_id=1, replica_groups={{0,1,2,3,16,17,18,19,32,33,34,35,48,49,50,51},{4,5,6,7,20,21,22,23,36,3..., dimensions={0} | all-to-all | bytes 5242880 | tf_op jit(solution)/shard_map/cond/branch_1_fun/all_to_all | solution.py:48
  135.2 3.9 %mix.5 = bf16[160,128]{1,0:T(8,128)(2,1)S(1)} custom-call(s32[1]{0:T(128)} %get-tuple-element.79.refs_0_, bf16[16,4,160,128]{3,2,1,0:T(8,128)(2,1)S(1)} %all_to_all.79.refs_1_, bf16[16,4,16,128]{3,2,1,0:T(8,128)(2,1)S(1)} %slice.80.refs_2_, bf16[3,4,4,4,128,128]{5,4,3,2,1,0:T(8,128)(2,1)S(1)} %bitcast.13, ...), custom_call_target="tpu_custom_call" | custom-call | tf_op jit(solution)/shard_map/cond/branch_1_fun/mix/pallas_call | solution.py:151
  139.1 9.9 %all_to_all.80 = bf16[4,160,128]{2,1,0:T(8,128)(2,1)S(1)} all-to-all(bf16[4,160,128]{2,1,0:T(8,128)(2,1)S(1)} %broadcast_in_dim.45), channel_id=1, replica_groups={{0,4,8,12},{1,5,9,13},{2,6,10,14},{3,7,11,15},{16,20,24,28},{17,21,25,2..., dimensions={0} | all-to-all | bytes 327680 | tf_op jit(solution)/shard_map/cond/branch_1_fun/all_to_all | solution.py:48
  149.6 23.0 %all_to_all.81.refs_1_ = bf16[16,4,160,128]{3,2,1,0:T(8,128)(2,1)S(1)} all-to-all(bf16[16,4,160,128]{3,2,1,0:T(8,128)(2,1)S(1)} %broadcast_in_dim.46), channel_id=1, replica_groups={{0,1,2,3,16,17,18,19,32,33,34,35,48,49,50,51},{4,5,6,7,20,21,22,23,36,3..., dimensions={0} | all-to-all | bytes 5242880 | tf_op jit(solution)/shard_map/cond/branch_1_fun/all_to_all | solution.py:48
  172.5 1.6 project_out.5
  174.4 1.3 collective-permute-start.5
  175.7 1.1 collective-permute-done.5
  176.8 23.9 %collective-permute-start.6 = (bf16[2,40,128]{2,1,0:T(8,128)(2,1)S(1)}, bf16[2,40,128]{2,1,0:T(8,128)(2,1)S(1)}, u32[]{:S(2)}, u32[]{:S(2)}) collective-permute-start(bf16[2,40,128]{2,1,0:T(8,128)(2,1)S(1)} %broadcast_select_fusion.3), channel_id=1, source_target_pairs={{0,64},{1,65},{2,66},{3,67},{4,68},{5,69},{6,70},{7,71},{8,72},{9,... | collective-permute-start | bytes 61448 | tf_op jit(solution)/shard_map/ppermute | solution.py:42
  200.7 0.8 collective-permute-done.6
  201.6 1.3 collective-permute-start.7
  202.9 152.8 %collective-permute-done.7 = bf16[2,40,128]{2,1,0:T(8,128)(2,1)S(1)} collective-permute-done((bf16[2,40,128]{2,1,0:T(8,128)(2,1)S(1)}, bf16[2,40,128]{2,1,0:T(8,128)(2,1)S(1)}, u32[]{:S(2)}, u32[]{:S(2)}) %collective-permute-start.7) | collective-permute-done | bytes 20512 | tf_op jit(solution)/shard_map/ppermute | solution.py:42
  355.7 0.6 maximum_select_fusion
  (47 shorter events, 1.8 us)
Async XLA Ops:
  0.0 6.1 %copy-start = (bf16[512,128]{1,0:T(8,128)(2,1)S(1)}, bf16[512,128]{1,0:T(8,128)(2,1)}, u32[]{:S(2)}) copy-start(bf16[512,128]{1,0:T(8,128)(2,1)} %param.17) | copy-start | bytes 393220
  2.2 4.4 %collective-permute-start.4 = (f32[32,128]{1,0:T(8,128)S(1)}, f32[32,128]{1,0:T(8,128)S(1)}, u32[]{:S(2)}, u32[]{:S(2)}) collective-permute-start(f32[32,128]{1,0:T(8,128)S(1)} %concatenate.21), channel_id=1, source_target_pairs={{0,64},{1,65},{2,66},{3,67},{4,68},{5,69},{6,70},{7,71},{8,72},{9,... | collective-permute-start | bytes 49160 | tf_op jit(solution)/shard_map/ppermute | solution.py:42
  8.6 48.9 %collective-permute-start.2 = (bf16[3,4,4,4,128,128]{5,4,3,2,1,0:T(8,128)(2,1)}, bf16[3,4,4,4,128,128]{5,4,3,2,1,0:T(8,128)(2,1)}, u32[]{:S(2)}, u32[]{:S(2)}) collective-permute-start(bf16[3,4,4,4,128,128]{5,4,3,2,1,0:T(8,128)(2,1)} %get-tuple-element.83.refs_3_), channel_id=1, source_target_pairs={{0,64},{1,65},{2,66},{3,67},{4,68},{5,69},{6,70},{7,71},{8,72},{9,... | collective-permute-start | bytes 18874376 | tf_op jit(solution)/shard_map/cond/branch_1_fun/ppermute | solution.py:42
  10.6 46.9 %collective-permute-start.3 = (bf16[4,4,4,128,128]{4,3,2,1,0:T(8,128)(2,1)}, bf16[4,4,4,128,128]{4,3,2,1,0:T(8,128)(2,1)}, u32[]{:S(2)}, u32[]{:S(2)}) collective-permute-start(bf16[4,4,4,128,128]{4,3,2,1,0:T(8,128)(2,1)} %get-tuple-element.84.refs_2_), channel_id=1, source_target_pairs={{0,64},{1,65},{2,66},{3,67},{4,68},{5,69},{6,70},{7,71},{8,72},{9,... | collective-permute-start | bytes 6291464 | tf_op jit(solution)/shard_map/cond/branch_1_fun/ppermute | solution.py:42
  75.0 23.9 %copy-start.3 = (bf16[4,4,4,128,128]{4,3,2,1,0:T(8,128)(2,1)S(1)}, bf16[4,4,4,128,128]{4,3,2,1,0:T(8,128)(2,1)}, u32[]{:S(2)}) copy-start(bf16[4,4,4,128,128]{4,3,2,1,0:T(8,128)(2,1)} %get-tuple-element.84.refs_2_) | copy-start | bytes 6291460 | tf_op jit(solution)/shard_map/cond
  98.9 36.3 %slice-start = ((s8[6291456]{0:T(1024)(128)(4,1)}), s8[4194304]{0:T(1024)(128)(4,1)S(1)}, s32[]{:S(2)}) async-start(s8[6291456]{0:T(1024)(128)(4,1)} %bitcast.12), calls=%async_computation.18 | async-start | bytes 8388608 | tf_op jit(solution)/shard_map/cond
  111.7 23.5 %slice-start.1 = ((s8[6291456]{0:T(1024)(128)(4,1)}), s8[2097152]{0:T(1024)(128)(4,1)S(1)}, s32[]{:S(2)}) async-start(s8[6291456]{0:T(1024)(128)(4,1)} %bitcast.12), calls=%async_computation.19 | async-start | bytes 4194304 | tf_op jit(solution)/shard_map/cond
  174.4 2.4 collective-permute-start.5
  176.8 179.5 %copy-start.1 = (bf16[512,128]{1,0:T(8,128)(2,1)S(1)}, bf16[512,128]{1,0:T(8,128)(2,1)}, u32[]{:S(2)}) copy-start(bf16[512,128]{1,0:T(8,128)(2,1)} %param.17) | copy-start | bytes 393220
  176.8 24.7 %collective-permute-start.6 = (bf16[2,40,128]{2,1,0:T(8,128)(2,1)S(1)}, bf16[2,40,128]{2,1,0:T(8,128)(2,1)S(1)}, u32[]{:S(2)}, u32[]{:S(2)}) collective-permute-start(bf16[2,40,128]{2,1,0:T(8,128)(2,1)S(1)} %broadcast_select_fusion.3), channel_id=1, source_target_pairs={{0,64},{1,65},{2,66},{3,67},{4,68},{5,69},{6,70},{7,71},{8,72},{9,... | collective-permute-start | bytes 61448 | tf_op jit(solution)/shard_map/ppermute | solution.py:42
  201.6 154.1 %collective-permute-start.7 = (bf16[2,40,128]{2,1,0:T(8,128)(2,1)S(1)}, bf16[2,40,128]{2,1,0:T(8,128)(2,1)S(1)}, u32[]{:S(2)}, u32[]{:S(2)}) collective-permute-start(bf16[2,40,128]{2,1,0:T(8,128)(2,1)S(1)} %pad_maximum_fusion.2), channel_id=1, source_target_pairs={{128,0},{129,1},{130,2},{131,3},{132,4},{133,5},{134,6},{135,7},{1... | collective-permute-start | bytes 61448 | tf_op jit(solution)/shard_map/ppermute | solution.py:42
